TPU v7x, 512 devices: a whole 4x8x8 slice. The times are simulated.
512 devices in a mesh: dp: 16 (over y_lo, x, core), ctx: 32 (over z, y_hi).
Axes of the slice: x: 4, y: 8 (y_hi: 4, y_lo: 2; y = y_hi * 2 + y_lo), z: 8, core: 2. Of those that a mesh axis runs over, the one named last changes fastest.
Arguments:
- frames: bfloat16 [16, 4096, 1024], P('dp', 'ctx'), may hold values from -64 to 64
- cotangent: bfloat16 [16, 4096, 1024], P('dp', 'ctx'), may hold values from -200 to 200
- lengths: int32 [16, 4], P('dp'), may hold values from 1 to 2048, 4096 in all within a row
- w_query: bfloat16 [1024, 512], P('dp'), may hold values from -8 to 8
- w_key: bfloat16 [1024, 512], P('dp'), may hold values from -8 to 8
- w_value: bfloat16 [1024, 512], P('dp'), may hold values from -0.1875 to 0.1875
- w_output: bfloat16 [512, 1024], P(None, 'dp'), may hold values from -1 to 1
- att_gain: float32 [1024], replicated, may hold values from 0.25 to 1.75
- conv_gain: float32 [1024], replicated, may hold values from 0.25 to 1.75
- kernel: float32 [9, 1024], replicated, may hold values from -2 to 2
- conv_bias: float32 [1024], replicated, may hold values from -3 to 3
Outputs:
- grad_frames: float32 [16, 4096, 1024], P('dp', 'ctx')
- grad_att_gain: float32 [1024], replicated
- grad_conv_gain: float32 [1024], replicated
- grad_kernel: float32 [9, 1024], replicated
- grad_bias: float32 [1024], replicated
Inputs may be any that keep to these rules, and one draw needn't show every extreme that they name: `lengths`: each row sums to 4096; its largest entry is exactly 2048.
All inputs are finite; a program needn't handle non-finite values.
Results may differ from a plain program's by a relative error of at most 0.012.
Values may be sent and summed in bfloat16 or wider, within the bound.
A program may use at most 64 MiB of HBM per device.

v0:
```python
import math

import jax
import jax.numpy as jnp
from jax import lax
from jax.sharding import PartitionSpec as P

HEAD_DIM = 128
HEADS = 4
LEFT = 128


epsilon = 1e-05


def shifted_2(block, axis, distance):
    devices = range(lax.axis_size(axis))
    route = [(i - distance, i) for i in devices if i - distance in devices]
    return lax.ppermute(block, axis, route)


def layer_norm(values, gain):
    center = values - jnp.mean(values, axis=-1, keepdims=True)
    inverse = lax.rsqrt(jnp.mean(center * center, axis=-1, keepdims=True) + epsilon)
    scaled = center * inverse
    return (scaled * gain, scaled, inverse)


def norm_back(grad_out, scaled, inverse, gain):
    grad_scaled = grad_out * gain
    first = jnp.mean(grad_scaled, axis=-1, keepdims=True)
    second = jnp.mean(grad_scaled * scaled, axis=-1, keepdims=True)
    return (inverse * (grad_scaled - first - scaled * second), jnp.sum(grad_out * scaled, axis=0))


def segment_of(places, bounds):
    return jnp.sum((bounds[None, :] <= places[:, None]).astype(jnp.int32), axis=1)


def band_mask(query_places, key_places, bounds):
    distance = query_places[:, None] - key_places[None, :]
    same = segment_of(query_places, bounds)[:, None] == segment_of(key_places, bounds)[None, :]
    return (distance >= 0) & (distance <= LEFT) & (key_places[None, :] >= 0) & same


def contract_last(left_side, right_side):
    return lax.dot_general(
        left_side, right_side, (((1,), (1,)), ((), ())), preferred_element_type=jnp.float32
    )


def windows(extended, first, block):
    count = block // LEFT
    lower = extended[first : first + block].reshape(count, LEFT, HEADS, HEAD_DIM)
    upper = extended[first + LEFT : first + LEFT + block].reshape(count, LEFT, HEADS, HEAD_DIM)
    return jnp.concatenate([lower, upper], axis=1)


def shards(
    frames,
    cotangent,
    lengths,
    w_query,
    w_key,
    w_value,
    w_output,
    att_gain,
    conv_gain,
    kernel,
    conv_bias,
):
    frame_rows = frames.shape[1]
    model_width = frames.shape[2]
    heads_width = w_query.shape[1]
    taps = kernel.shape[0]
    block = math.gcd(frame_rows, 512)
    count = block // LEFT
    scale = HEAD_DIM ** (-0.5)
    offset = lax.axis_index("ctx") * frame_rows
    places = offset + jnp.arange(frame_rows, dtype=jnp.int32)
    bounds = jnp.cumsum(lengths[0])
    segments = segment_of(places, bounds)
    banded = jax.vmap(band_mask, in_axes=(0, 0, None))
    inputs = frames[0].astype(jnp.float32)
    norm_a, scaled_a, inverse_a = layer_norm(inputs, att_gain)
    norm_ab = norm_a.astype(jnp.bfloat16)
    pieces = (
        lax.all_gather(w_query, "dp", axis=0, tiled=True),
        lax.all_gather(w_key, "dp", axis=0, tiled=True),
        lax.all_gather(w_value, "dp", axis=0, tiled=True),
    )
    part = norm_ab
    query, keys, values = tuple(
        (jnp.dot(part, piece, preferred_element_type=jnp.float32) for piece in pieces)
    )
    query = query.astype(jnp.bfloat16)
    keys = keys.astype(jnp.bfloat16)
    values = values.astype(jnp.bfloat16)
    key_rim, value_rim = shifted_2((keys, values), "ctx", 1)
    keys_ext = jnp.concatenate([key_rim, keys], axis=0)
    values_ext = jnp.concatenate([value_rim, values], axis=0)
    window_offsets = (jnp.arange(count, dtype=jnp.int32) * LEFT)[:, None] + jnp.arange(
        2 * LEFT, dtype=jnp.int32
    )[None, :]
    block_index = 0
    first = block_index * block
    query_places = places.reshape(count, LEFT)
    key_places = offset + first - LEFT + window_offsets
    allowed = banded(query_places, key_places, bounds)
    heads_q = query.reshape(count, LEFT, HEADS, HEAD_DIM)
    scores = jnp.einsum(
        "sqhd,skhd->shqk",
        heads_q,
        windows(keys_ext, first, block),
        preferred_element_type=jnp.float32,
    )
    scores = jnp.where(allowed[:, None], scores * scale, -jnp.inf)
    row_max = jnp.max(scores, axis=-1, keepdims=True)
    shifted = jnp.exp(scores - row_max)
    total = jnp.sum(shifted, axis=-1, keepdims=True)
    probs = shifted / total
    probs_b = probs.astype(jnp.bfloat16)
    context = jnp.einsum(
        "shqk,skhd->sqhd",
        probs_b,
        windows(values_ext, first, block),
        preferred_element_type=jnp.float32,
    )
    saved = [(probs, probs_b)]
    contexts = context.reshape(block, heads_width).astype(jnp.bfloat16)
    context = contexts
    attended = jnp.dot(
        context,
        lax.all_gather(w_output, "dp", axis=1, tiled=True),
        preferred_element_type=jnp.float32,
    )
    mid = inputs + attended
    norm_c, scaled_c, inverse_c = layer_norm(mid, conv_gain)
    conv_in = norm_c.astype(jnp.bfloat16)
    conv_rim = shifted_2(conv_in[frame_rows - taps + 1 :], "ctx", 1)
    conv_pad = jnp.concatenate([conv_rim, conv_in], axis=0)
    conv = jnp.zeros((frame_rows, model_width), jnp.float32) + conv_bias
    tap_masks = []
    for tap in range(taps):
        sources = places - taps + 1 + tap
        valid = ((sources >= 0) & (segment_of(sources, bounds) == segments))[:, None]
        tap_masks.append(valid)
        conv = conv + jnp.where(
            valid, kernel[tap] * conv_pad[tap : tap + frame_rows].astype(jnp.float32), 0.0
        )
    grad_out = cotangent[0].astype(jnp.float32)
    gate_value = jax.nn.sigmoid(conv)
    grad_conv = grad_out * gate_value * (1.0 + conv * (1.0 - gate_value))
    grad_bias = jnp.sum(grad_conv, axis=0)
    kernel_rows = []
    grad_pad = jnp.zeros((frame_rows + taps - 1, model_width), jnp.float32)
    for tap in range(taps):
        kept = jnp.where(tap_masks[tap], grad_conv, 0.0)
        kernel_rows.append(
            jnp.sum(kept * conv_pad[tap : tap + frame_rows].astype(jnp.float32), axis=0)
        )
        grad_pad = grad_pad.at[tap : tap + frame_rows].add(kernel[tap] * kept)
    grad_kernel = jnp.stack(kernel_rows)
    conv_back = shifted_2(grad_pad[: taps - 1].astype(jnp.bfloat16), "ctx", -1).astype(jnp.float32)
    grad_conv_in = grad_pad[taps - 1 :].at[frame_rows - taps + 1 :].add(conv_back)
    grad_mid_norm, grad_conv_gain = norm_back(grad_conv_in, scaled_c, inverse_c, conv_gain)
    grad_mid = grad_out + grad_mid_norm
    grad_mid_b = grad_mid.astype(jnp.bfloat16)
    part = grad_mid_b
    grad_context = contract_last(part, lax.all_gather(w_output, "dp", axis=1, tiled=True))
    grad_context = grad_context.astype(jnp.bfloat16)
    grad_keys_ext = jnp.zeros((LEFT + frame_rows, heads_width), jnp.float32)
    grad_values_ext = jnp.zeros((LEFT + frame_rows, heads_width), jnp.float32)
    block_index = 0
    first = block_index * block
    probs, probs_b = saved[block_index]
    heads_q = query.reshape(count, LEFT, HEADS, HEAD_DIM)
    heads_g = grad_context.reshape(count, LEFT, HEADS, HEAD_DIM)
    grad_probs = jnp.einsum(
        "sqhd,skhd->shqk",
        heads_g,
        windows(values_ext, first, block),
        preferred_element_type=jnp.float32,
    )
    delta = jnp.sum(probs * grad_probs, axis=-1, keepdims=True)
    grad_scores = (probs * (grad_probs - delta) * scale).astype(jnp.bfloat16)
    query_part = jnp.einsum(
        "shqk,skhd->sqhd",
        grad_scores,
        windows(keys_ext, first, block),
        preferred_element_type=jnp.float32,
    )
    query_grads = query_part.reshape(block, heads_width).astype(jnp.bfloat16)
    key_part = jnp.einsum(
        "shqk,sqhd->skhd", grad_scores, heads_q, preferred_element_type=jnp.float32
    ).reshape(count, 2 * LEFT, heads_width)
    value_part = jnp.einsum(
        "shqk,sqhd->skhd", probs_b, heads_g, preferred_element_type=jnp.float32
    ).reshape(count, 2 * LEFT, heads_width)
    grad_keys_ext = grad_keys_ext.at[first : first + block].add(
        key_part[:, :LEFT].reshape(block, heads_width)
    )
    grad_keys_ext = grad_keys_ext.at[first + LEFT : first + LEFT + block].add(
        key_part[:, LEFT:].reshape(block, heads_width)
    )
    grad_values_ext = grad_values_ext.at[first : first + block].add(
        value_part[:, :LEFT].reshape(block, heads_width)
    )
    grad_values_ext = grad_values_ext.at[first + LEFT : first + LEFT + block].add(
        value_part[:, LEFT:].reshape(block, heads_width)
    )
    key_back, value_back = (
        shifted_2(grad_keys_ext[:LEFT].astype(jnp.bfloat16), "ctx", -1).astype(jnp.float32),
        shifted_2(grad_values_ext[:LEFT].astype(jnp.bfloat16), "ctx", -1).astype(jnp.float32),
    )
    grad_key = grad_keys_ext[LEFT:].at[frame_rows - LEFT :].add(key_back).astype(jnp.bfloat16)
    grad_value = grad_values_ext[LEFT:].at[frame_rows - LEFT :].add(value_back).astype(jnp.bfloat16)
    pieces = lax.all_gather((w_query, w_key, w_value), "dp", axis=0, tiled=True)
    total = contract_last(query_grads, pieces[0]) + contract_last(grad_key, pieces[1])
    grad_norm_a = total + contract_last(grad_value, pieces[2])
    grad_input_norm, grad_att_gain = norm_back(grad_norm_a, scaled_a, inverse_a, att_gain)
    grad_frames = (grad_mid_norm + grad_input_norm)[None]
    grad_kernel, grad_bias, grad_conv_gain, grad_att_gain = lax.psum(
        (grad_kernel, grad_bias, grad_conv_gain, grad_att_gain), ("dp", "ctx")
    )
    factor = 1.0 / math.sqrt(
        lax.axis_size("dp") * frames.shape[0] * frame_rows * lax.axis_size("ctx")
    )
    return (
        grad_frames,
        grad_att_gain * factor,
        grad_conv_gain * factor,
        grad_kernel * factor,
        grad_bias * factor,
    )


def solution(mesh):
    return jax.shard_map(
        shards,
        mesh=mesh,
        in_specs=(
            P("dp", "ctx", None),
            P("dp", "ctx", None),
            P("dp", None),
            P("dp", None),
            P("dp", None),
            P("dp", None),
            P(None, "dp"),
            P(),
            P(),
            P(),
            P(),
        ),
        out_specs=(P("dp", "ctx", None), P(), P(), P(), P()),
        check_vma=False,
    )
```

profile of v0, /device:TPU:1, one launch (start us, length us, event | category | flops | bytes accessed | tf_op | source)
XLA Modules:
  0.0 339.3 jit_solution(8674582719469220419)
XLA Ops:
  11.5 42.3 %all-gather.5.cloned.1.call-done = bf16[1024,512]{1,0:T(8,128)(2,1)} async-done(((bf16[64,512]{1,0:T(8,128)(2,1)}), bf16[1024,512]{1,0:T(8,128)(2,1)}) %all-gather.5.cloned.1.call-update) | async-done | bytes 1048592 | tf_op jit(solution)/shard_map/all_gather | solution.py:90
  53.8 1.6 convolution_convert_fusion.5
  55.5 4.0 %collective-permute-start = (bf16[128,512]{1,0:T(8,128)(2,1)S(1)}, bf16[128,512]{1,0:T(8,128)(2,1)S(1)}, u32[]{:S(2)}, u32[]{:S(2)}) collective-permute-start(bf16[128,512]{1,0:T(8,128)(2,1)S(1)} %convolution_convert_fusion.5), channel_id=1, source_target_pairs={{0,1},{1,2},{2,3},{3,4},{4,5},{5,6},{6,7},{7,8},{8,9},{9,10},{10,1... | collective-permute-start | bytes 393224 | tf_op jit(solution)/shard_map/ppermute | solution.py:19
  59.6 34.2 %all-gather.9.cloned.1.call-done = bf16[1024,512]{1,0:T(8,128)(2,1)} async-done(((bf16[64,512]{1,0:T(8,128)(2,1)}), bf16[1024,512]{1,0:T(8,128)(2,1)}) %all-gather.9.cloned.1.call-update) | async-done | bytes 1048592 | tf_op jit(solution)/shard_map/all_gather | solution.py:89
  93.8 1.6 convolution_convert_fusion.3
  95.4 4.0 %collective-permute-start.1 = (bf16[128,512]{1,0:T(8,128)(2,1)S(1)}, bf16[128,512]{1,0:T(8,128)(2,1)S(1)}, u32[]{:S(2)}, u32[]{:S(2)}) collective-permute-start(bf16[128,512]{1,0:T(8,128)(2,1)S(1)} %convolution_convert_fusion.3), channel_id=1, source_target_pairs={{0,1},{1,2},{2,3},{3,4},{4,5},{5,6},{6,7},{7,8},{8,9},{9,10},{10,1... | collective-permute-start | bytes 393224 | tf_op jit(solution)/shard_map/ppermute | solution.py:19
  99.5 34.3 %all-gather.7.cloned.1.call-done = bf16[1024,512]{1,0:T(8,128)(2,1)} async-done(((bf16[64,512]{1,0:T(8,128)(2,1)}), bf16[1024,512]{1,0:T(8,128)(2,1)}) %all-gather.7.cloned.1.call-update) | async-done | bytes 1048592 | tf_op jit(solution)/shard_map/all_gather | solution.py:88
  133.8 1.6 convolution_convert_fusion.4
  135.8 1.2 fusion.103
  138.1 35.6 %all-gather.11.cloned.1.call-done = bf16[512,1024]{0,1:T(8,128)(2,1)} async-done(((bf16[512,64]{0,1:T(8,128)(2,1)}), bf16[512,1024]{0,1:T(8,128)(2,1)}) %all-gather.11.cloned.1.call-update) | async-done | bytes 1048592 | tf_op jit(solution)/shard_map/all_gather | solution.py:134
  173.7 1.8 fusion.104
  176.7 4.0 %collective-permute-start.2 = (bf16[8,1024]{1,0:T(8,128)(2,1)S(1)}, bf16[8,1024]{1,0:T(8,128)(2,1)S(1)}, u32[]{:S(2)}, u32[]{:S(2)}) collective-permute-start(bf16[8,1024]{1,0:T(8,128)(2,1)S(1)} %slice.407), channel_id=1, source_target_pairs={{0,1},{1,2},{2,3},{3,4},{4,5},{5,6},{6,7},{7,8},{8,9},{9,10},{10,1... | collective-permute-start | bytes 49160 | tf_op jit(solution)/shard_map/ppermute | solution.py:19
  182.3 1.5 fusion.51
  188.3 1.3 collective-permute-start.3
  190.5 1.3 stack.39
  191.8 2.6 collective-permute-done.3
  197.8 4.8 %convolution_convert_fusion = bf16[4,128,128]{2,1,0:T(8,128)(2,1)} fusion(f32[4,128,256]{2,1,0:T(8,128)S(1)} %fusion.73, bf16[1,128,4,128]{3,1,2,0:T(8,128)(2,1)S(1)} %copy-done.13, bf16[1,128,4,128]{3,1,2,0:T(8,128)(2,1)S(1)} %copy-done.17, f32[4,128,256]{2,1,0:T(8,128)} %get-tuple-element.261, f32[4,128]{1,0:T(4,128)S(1)} %copy-done.40), kind=kOutput, calls=%fused_computation.13 | convolution fusion | flops 35062528 | bytes 1443840 | tf_op jit(solution)/shard_map/shqk,skhd->sqhd/dot_general | solution.py:187
  202.6 3.7 %fusion.9 = f32[4,128,256]{2,1,0:T(8,128)S(1)} fusion(bf16[128,4,128]{0,2,1:T(8,128)(2,1)S(1)} %bitcast.163, f32[4,128,256]{2,1,0:T(8,128)S(1)} %fusion.73, f32[4,128,256]{2,1,0:T(8,128)} %get-tuple-element.261, f32[4,128]{1,0:T(4,128)S(1)} %copy-done.40), kind=kOutput, calls=%fused_computation.19 | convolution fusion | flops 34472704 | bytes 1705984 | tf_op jit(solution)/shard_map/shqk,sqhd->skhd/dot_general | solution.py:194
  206.3 1.7 fusion.78
  208.1 1.4 collective-permute-start.5
  209.6 1.5 collective-permute-start.4
  211.6 14.0 %collective-permute-done.4 = bf16[128,512]{0,1:T(8,128)(2,1)S(1)} collective-permute-done((bf16[128,512]{0,1:T(8,128)(2,1)S(1)}, bf16[128,512]{0,1:T(8,128)(2,1)S(1)}, u32[]{:S(2)}, u32[]{:S(2)}) %collective-permute-start.4) | collective-permute-done | bytes 131104 | tf_op jit(solution)/shard_map/ppermute | solution.py:19
  226.9 101.6 %all-reduce.1 = (f32[1024]{0:T(1024)S(1)}, f32[1024]{0:T(1024)S(1)}, f32[9,1024]{1,0:T(8,128)S(1)}, f32[1024]{0:T(1024)S(1)}) all-reduce(f32[1024]{0:T(1024)S(1)} %get-tuple-element.223, f32[1024]{0:T(1024)S(1)} %get-tuple-element.213, f32[9,1024]{1,0:T(8,128)S(1)} %copy-done.11, ...), channel_id=1, replica_groups=mesh['dp'=16,'ctx'=32] {'dp','ctx'}, use_global_device_ids=true, to_apply=%region_24.25 | all-reduce | flops 12288 | bytes 98304 | tf_op jit(solution)/shard_map/psum | solution.py:223
  331.6 1.1 fusion.26
  (163 shorter events, 22.1 us)
Async XLA Ops:
  7.2 46.6 %all-gather.5.cloned.1.call-start = ((), (), s32[]{:S(2)}) async-start(), calls=%async_computation | async-start | bytes 1114112 | tf_op jit(solution)/shard_map/all_gather | solution.py:90
  7.9 85.9 %all-gather.9.cloned.1.call-start = ((), (), s32[]{:S(2)}) async-start(), calls=%async_computation.2 | async-start | bytes 1114112 | tf_op jit(solution)/shard_map/all_gather | solution.py:89
  8.7 125.1 %all-gather.7.cloned.1.call-start = ((), (), s32[]{:S(2)}) async-start(), calls=%async_computation.1 | async-start | bytes 1114112 | tf_op jit(solution)/shard_map/all_gather | solution.py:88
  9.4 164.3 %all-gather.11.cloned.1.call-start = ((), (), s32[]{:S(2)}) async-start(), calls=%async_computation.3 | async-start | bytes 1114112 | tf_op jit(solution)/shard_map/all_gather | solution.py:134
  10.2 123.6 %copy-start.29 = (f32[128]{0:T(128)}, f32[128]{0:T(128)S(1)}, u32[]{:S(2)}) copy-start(f32[128]{0:T(128)S(1)} %broadcast_multiply_fusion.9) | copy-start | bytes 1540
  10.4 123.4 %copy-start.32 = (f32[128]{0:T(128)}, f32[128]{0:T(128)S(1)}, u32[]{:S(2)}) copy-start(f32[128]{0:T(128)S(1)} %add_rsqrt_fusion.1) | copy-start | bytes 1540
  11.5 125.5 %copy-start.20 = (pred[128,256]{1,0:T(8,128)(4,1)}, pred[128,256]{1,0:T(8,128)(4,1)S(1)}, u32[]{:S(2)}) copy-start(pred[128,256]{1,0:T(8,128)(4,1)S(1)} %fusion.83) | copy-start | bytes 98308
  11.5 42.3 %copy-start.22 = (f32[1024]{0:T(1024)S(1)}, f32[1024]{0:T(1024)}, u32[]{:S(2)}) copy-start(f32[1024]{0:T(1024)} %param.54) | copy-start | bytes 12292
  55.5 81.4 %copy-start.7 = (bf16[128,512]{0,1:T(8,128)(2,1)}, bf16[128,512]{0,1:T(8,128)(2,1)S(1)}, u32[]{:S(2)}) copy-start(bf16[128,512]{0,1:T(8,128)(2,1)S(1)} %copy.39) | copy-start | bytes 393220
  55.5 80.1 %collective-permute-start = (bf16[128,512]{1,0:T(8,128)(2,1)S(1)}, bf16[128,512]{1,0:T(8,128)(2,1)S(1)}, u32[]{:S(2)}, u32[]{:S(2)}) collective-permute-start(bf16[128,512]{1,0:T(8,128)(2,1)S(1)} %convolution_convert_fusion.5), channel_id=1, source_target_pairs={{0,1},{1,2},{2,3},{3,4},{4,5},{5,6},{6,7},{7,8},{8,9},{9,10},{10,1... | collective-permute-start | bytes 393224 | tf_op jit(solution)/shard_map/ppermute | solution.py:19
  95.4 40.1 %collective-permute-start.1 = (bf16[128,512]{1,0:T(8,128)(2,1)S(1)}, bf16[128,512]{1,0:T(8,128)(2,1)S(1)}, u32[]{:S(2)}, u32[]{:S(2)}) collective-permute-start(bf16[128,512]{1,0:T(8,128)(2,1)S(1)} %convolution_convert_fusion.3), channel_id=1, source_target_pairs={{0,1},{1,2},{2,3},{3,4},{4,5},{5,6},{6,7},{7,8},{8,9},{9,10},{10,1... | collective-permute-start | bytes 393224 | tf_op jit(solution)/shard_map/ppermute | solution.py:19
  99.5 37.4 %copy-start.12 = (bf16[1,128,4,128]{3,1,2,0:T(8,128)(2,1)}, bf16[1,128,4,128]{3,1,2,0:T(8,128)(2,1)S(1)}, u32[]{:S(2)}) copy-start(bf16[1,128,4,128]{3,1,2,0:T(8,128)(2,1)S(1)} %copy.29) | copy-start | bytes 393220
  176.5 5.1 %copy-start.5 = (bf16[1,128,1024]{2,1,0:T(8,128)(2,1)S(1)}, bf16[1,128,1024]{2,1,0:T(8,128)(2,1)}, u32[]{:S(2)}) copy-start(bf16[1,128,1024]{2,1,0:T(8,128)(2,1)} %param.48) | copy-start | bytes 786436
  176.7 4.9 %collective-permute-start.2 = (bf16[8,1024]{1,0:T(8,128)(2,1)S(1)}, bf16[8,1024]{1,0:T(8,128)(2,1)S(1)}, u32[]{:S(2)}, u32[]{:S(2)}) collective-permute-start(bf16[8,1024]{1,0:T(8,128)(2,1)S(1)} %slice.407), channel_id=1, source_target_pairs={{0,1},{1,2},{2,3},{3,4},{4,5},{5,6},{6,7},{7,8},{8,9},{9,10},{10,1... | collective-permute-start | bytes 49160 | tf_op jit(solution)/shard_map/ppermute | solution.py:19
  188.3 6.0 %collective-permute-start.3 = (bf16[8,1024]{1,0:T(8,128)(2,1)S(1)}, bf16[8,1024]{1,0:T(8,128)(2,1)S(1)}, u32[]{:S(2)}, u32[]{:S(2)}) collective-permute-start(bf16[8,1024]{1,0:T(8,128)(2,1)S(1)} %slice.549), channel_id=1, source_target_pairs={{1,0},{2,1},{3,2},{4,3},{5,4},{6,5},{7,6},{8,7},{9,8},{10,9},{11,1... | collective-permute-start | bytes 49160 | tf_op jit(solution)/shard_map/ppermute | solution.py:19
  190.3 4.8 %copy-start.1 = (bf16[512,1024]{0,1:T(8,128)(2,1)S(1)}, bf16[512,1024]{0,1:T(8,128)(2,1)}, u32[]{:S(2)}) copy-start(bf16[512,1024]{0,1:T(8,128)(2,1)} %all-gather.11.cloned.1.call-done) | copy-start | bytes 3145732
  197.8 4.8 %copy-start.15 = (bf16[128,512]{0,1:T(8,128)(2,1)S(1)}, bf16[128,512]{0,1:T(8,128)(2,1)}, u32[]{:S(2)}) copy-start(bf16[128,512]{0,1:T(8,128)(2,1)} %copy-done.14) | copy-start | bytes 393220
  206.3 4.7 %copy-start.4 = (bf16[1024,512]{1,0:T(8,128)(2,1)S(1)}, bf16[1024,512]{1,0:T(8,128)(2,1)}, u32[]{:S(2)}) copy-start(bf16[1024,512]{1,0:T(8,128)(2,1)} %all-gather.7.cloned.1.call-done) | copy-start | bytes 3145732
  208.1 17.4 %copy-start.3 = (bf16[1024,512]{1,0:T(8,128)(2,1)S(1)}, bf16[1024,512]{1,0:T(8,128)(2,1)}, u32[]{:S(2)}) copy-start(bf16[1024,512]{1,0:T(8,128)(2,1)} %all-gather.9.cloned.1.call-done) | copy-start | bytes 3145732
  208.1 17.9 %collective-permute-start.5 = (bf16[128,512]{0,1:T(8,128)(2,1)S(1)}, bf16[128,512]{0,1:T(8,128)(2,1)S(1)}, u32[]{:S(2)}, u32[]{:S(2)}) collective-permute-start(bf16[128,512]{0,1:T(8,128)(2,1)S(1)} %fusion.77), channel_id=1, source_target_pairs={{1,0},{2,1},{3,2},{4,3},{5,4},{6,5},{7,6},{8,7},{9,8},{10,9},{11,1... | collective-permute-start | bytes 393224 | tf_op jit(solution)/shard_map/ppermute | solution.py:19
  209.6 16.0 %collective-permute-start.4 = (bf16[128,512]{0,1:T(8,128)(2,1)S(1)}, bf16[128,512]{0,1:T(8,128)(2,1)S(1)}, u32[]{:S(2)}, u32[]{:S(2)}) collective-permute-start(bf16[128,512]{0,1:T(8,128)(2,1)S(1)} %fusion.75), channel_id=1, source_target_pairs={{1,0},{2,1},{3,2},{4,3},{5,4},{6,5},{7,6},{8,7},{9,8},{10,9},{11,1... | collective-permute-start | bytes 393224 | tf_op jit(solution)/shard_map/ppermute | solution.py:19
  211.5 14.5 %copy-start.2 = (bf16[1024,512]{1,0:T(8,128)(2,1)S(1)}, bf16[1024,512]{1,0:T(8,128)(2,1)}, u32[]{:S(2)}) copy-start(bf16[1024,512]{1,0:T(8,128)(2,1)} %all-gather.5.cloned.1.call-done) | copy-start | bytes 3145732
  211.6 14.5 %copy-start.30 = (f32[128]{0:T(128)S(1)}, f32[128]{0:T(128)}, u32[]{:S(2)}) copy-start(f32[128]{0:T(128)} %copy-done.29) | copy-start | bytes 1540
  211.6 14.5 %copy-start.33 = (f32[128]{0:T(128)S(1)}, f32[128]{0:T(128)}, u32[]{:S(2)}) copy-start(f32[128]{0:T(128)} %copy-done.32) | copy-start | bytes 1540
  (27 other events, 30.2 us)
Sparse Core Ops, SparseCore 0:
  10.2 43.6 all-gather.4
  55.9 37.8 all-gather.8
  95.9 37.8 all-gather.6
  135.8 37.8 all-gather.10
where the time goes:
time: 340 us; the launch traced here: 339 us
  waiting for transfers between devices  166 us (49%)
  blocking collectives  102 us (30%)
  matrix products  20.7 us (6%)
  starting transfers between devices  16.5 us (5%)
  between operations  14.5 us (4%)
  local copies, waits for them, and re-layouts  11 us (3%)
  other arithmetic  8.58 us (3%)
    psum x1, blocking collectives, shards(): lax.psum((grad_kernel, grad_bias, grad_conv_gain, grad_att_gain), ('dp',...  102 us
    all_gather x1, waiting for transfers between devices, shards(): lax.all_gather(w_value, 'dp', axis=0, tiled=True)  42.3 us
    all_gather x1, waiting for transfers between devices, shards(): lax.all_gather(w_output, 'dp', axis=1, tiled=True)  35.6 us
    all_gather x1, waiting for transfers between devices, shards(): lax.all_gather(w_query, 'dp', axis=0, tiled=True)  34.3 us
    all_gather x1, waiting for transfers between devices, shards(): lax.all_gather(w_key, 'dp', axis=0, tiled=True)  34.2 us
    ppermute x6, waiting for transfers between devices, shifted_2(): return lax.ppermute(block, axis, route)  17.4 us
    ppermute x6, starting transfers between devices, shifted_2(): return lax.ppermute(block, axis, route)  16.3 us
  transfers between devices with their start and end apart: 10, of which 7 were waited for; matrix products, arithmetic and copies ran while one was open for 3% of the time, Pallas kernels for 0%

commit v1 on v0

v1 whole, which is shorter than its diff:
```python
import math

import jax
import jax.numpy as jnp
from jax import lax
from jax.experimental import pallas as pl
from jax.experimental.pallas import tpu as pltpu
from jax.sharding import PartitionSpec as P

MESH = pl.DeviceIdType.MESH
NX, NY, NZ = 4, 8, 8
ROWS = 128
WIDTH = 1024
HEADS = 4
HEAD_DIM = 128
HEADS_WIDTH = HEADS * HEAD_DIM
LEFT = 128
TAPS = 9
RIM = 16
EXT = 2 * ROWS + 2 * RIM
CONV = ROWS + 16
DEEP = 64
GROUP = 8
EPSILON = 1e-05
FAR = -1e30
BEFORE = -(1 << 20)
SCALE = HEAD_DIM ** (-0.5)
SLOTS = 176
F32 = jnp.float32
BF16 = jnp.bfloat16

SHARDS = ((-1, 0), (1, 0), (2, 0), (0, 1), (-1, 1), (1, 1), (2, 1))


class Links:
    def __init__(self, send_sems, recv_sems):
        self.send_sems, self.recv_sems = send_sems, recv_sems
        self.names, self.sent = {}, []

    def copy(self, name, source, target, device):
        slot = self.names.setdefault(name, len(self.names))
        assert slot < SLOTS
        return pltpu.make_async_remote_copy(
            src_ref=source,
            dst_ref=target,
            send_sem=self.send_sems.at[slot],
            recv_sem=self.recv_sems.at[slot],
            device_id=device,
            device_id_type=MESH,
        )

    def send(self, name, source, target, device):
        copy = self.copy(name, source, target, device)
        copy.start()
        self.sent.append(copy)

    def arrived(self, name, target, device):
        self.copy(name, target, target, device).wait_recv()

    def finish(self):
        for copy in self.sent:
            copy.wait_send()


def dot(left, right):
    return jnp.dot(left, right, preferred_element_type=F32)


def dot_nt(left, right):
    return lax.dot_general(left, right, (((1,), (1,)), ((), ())), preferred_element_type=F32)


def dot_tn(left, right):
    return lax.dot_general(left, right, (((0,), (0,)), ((), ())), preferred_element_type=F32)


def normalize(values):
    center = values - jnp.mean(values, axis=-1, keepdims=True)
    inverse = lax.rsqrt(jnp.mean(center * center, axis=-1, keepdims=True) + EPSILON)
    return center * inverse, inverse


def wide(column, width):
    return jnp.broadcast_to(column, (column.shape[0], width))


def spread(block):
    return jnp.concatenate([block] * (WIDTH // 128), axis=1)


def iota(shape, axis):
    return lax.broadcasted_iota(jnp.int32, shape, axis)


def block_kernel(
    frames, cotangent, lengths, w_query, w_key, w_value, w_output, att_gain, conv_gain, kernel, bias,
    out_frames, out_att, out_conv, out_kernel, out_bias,
    xs, cts, weights, w_in, gain_a, gain_c, taps_ref, bias_ref,
    norm_b, scaled_a, inverse_a, keys, values, query, query_e, query_n, probs, context, mid,
    scaled_c, inverse_c, conv_in, age, grad_conv, grad_conv_in, grad_mid_norm, grad_mid_b,
    grad_context, grad_context_n, grad_query, grad_key, grad_value, grad_key_f, grad_value_f, grad_norm_a,
    frames_out, mask_main, mask_rim, mask_next, stats, stats_n, delta, delta_n,
    early, early_x, early_y, early_z, early_all, late_sum, late_x, late_y, late_z,
    att_row, conv_row, kernel_rows, bias_row,
    send_sems, recv_sems, local_sems,
):
    dp, ctx = lax.axis_index("dp"), lax.axis_index("ctx")
    core = lax.rem(dp, 2)
    x = lax.rem(lax.div(dp, 2), NX)
    y_lo = lax.div(dp, 2 * NX)
    z = lax.div(ctx, NY // 2)
    y = lax.rem(ctx, NY // 2) * 2 + y_lo
    offset = ctx * ROWS
    group = x * 2 + core

    def at(px, py, pz, pc):
        return ((lax.rem(py, 2) * NX + px) * 2 + pc, pz * (NY // 2) + lax.div(py, 2))

    def shift(value, step, size):
        return lax.rem(value + (step + size), size)

    def frames_at(step):
        return (dp, shift(ctx, step, 4 * NZ))

    sibling = (dp + 1 - 2 * core, ctx)
    right, left = at(shift(x, 1, NX), y, z, core), at(shift(x, -1, NX), y, z, core)
    above, below = at(x, shift(y, 1, NY), z, core), at(x, shift(y, -1, NY), z, core)
    front, back = at(x, y, shift(z, 1, NZ), core), at(x, y, shift(z, -1, NZ), core)
    later, earlier, later_2 = frames_at(1), frames_at(-1), frames_at(2)

    def group_peer(step):
        other = shift(group, step, GROUP)
        return other, at(lax.div(other, 2), y, z, lax.rem(other, 2))

    def y_peer(step):
        other = shift(y, step, NY)
        return other, at(x, other, z, core)

    def z_peer(step):
        other = shift(z, step, NZ)
        return other, at(x, y, other, core)

    links = Links(send_sems, recv_sems)
    local = []

    def bring(source, target):
        copy = pltpu.make_async_copy(source, target, local_sems.at[len(local)])
        copy.start()
        local.append(copy)
        return copy

    own_rows = pl.ds(pl.multiple_of(dp * DEEP, DEEP), DEEP)
    got_output = bring(w_output, w_in)
    got_weights = [
        bring(source, weights.at[index, own_rows, :])
        for index, source in ((0, w_key), (1, w_value), (2, w_query))
    ]
    got_frames = bring(frames.at[0], xs.at[pl.ds(0, ROWS), :])
    got_rest = [
        bring(cotangent.at[0], cts.at[pl.ds(0, ROWS), :]),
        bring(att_gain, gain_a),
        bring(conv_gain, gain_c),
        bring(kernel, taps_ref),
        bring(bias, bias_ref),
    ]

    barrier = pltpu.get_barrier_semaphore()
    peers = [group_peer(step)[1] for step in range(1, GROUP)]
    peers += [y_peer(step)[1] for step in range(1, NY)]
    peers += [z_peer(step)[1] for step in range(1, NZ)]
    peers += [later, earlier, later_2, frames_at(-2)]
    for peer in peers:
        pl.semaphore_signal(barrier, inc=1, device_id=peer, device_id_type=MESH)
    got_output.wait()
    weights[3, own_rows, :] = w_in[...].astype(F32).T.astype(BF16)
    for copy in got_weights:
        copy.wait()
    pl.semaphore_wait(barrier, len(peers))

    links.send("prev", frames.at[0], xs.at[pl.ds(ROWS, ROWS), :], later)
    links.send("next", frames.at[0, pl.ds(0, RIM), :], xs.at[pl.ds(2 * ROWS + RIM, RIM), :], earlier)
    links.send("prev2", frames.at[0, pl.ds(ROWS - RIM, RIM), :], xs.at[pl.ds(2 * ROWS, RIM), :], later_2)
    links.send("cot", cotangent.at[0, pl.ds(0, RIM), :], cts.at[pl.ds(ROWS, RIM), :], earlier)

    half = lax.rem(z, 2)

    def shard(index, of_core):
        if index is None:
            return (y_lo * NX + x) * 2 + of_core
        step, other = SHARDS[index]
        side = 1 - y_lo if other else y_lo
        return (side * NX + shift(x, step, NX)) * 2 + of_core

    def piece(index, of_half, part, wave, of_core):
        first, size = shard(index, of_core) * DEEP, DEEP
        if of_half is not None:
            first, size = first + of_half * 32, 32
        if part is not None:
            first, size = first + part * 16, 16
        return weights.at[pl.ds(2 * wave, 2), pl.ds(pl.multiple_of(first, 16), size), :]

    def give(name, index, of_half, part, wave, device):
        ref = piece(index, of_half, part, wave, core)
        links.send((name, wave), ref, ref, device)

    def take(name, index, of_half, part, wave, of_core=None):
        ref = piece(index, of_half, part, wave, core if of_core is None else of_core)
        links.arrived((name, wave), ref, sibling)

    siblings = []

    def pass_on(name, index, of_half, part, wave):
        give("sib" + name, index, of_half, part, wave, sibling)
        siblings.append((name, index, of_half, part, wave))

    def pass_z(index, parts, wave):
        for part in parts:
            give(f"z{part}{index}", index, half, part, wave, (front, back)[part])

    for wave in (0, 1):
        give("0", None, half, None, wave, right)
        give("1", None, half, None, wave, left)
        give("3", None, half, None, wave, below)
        pass_on("own", None, None, None, wave)

    got_frames.wait()
    for copy in got_rest:
        copy.wait()

    def norm_rows(first, size, own):
        block = xs[pl.ds(first, size), :].astype(F32)
        scaled, inverse = normalize(block)
        norm_b[pl.ds(first, size), :] = (scaled * gain_a[...]).astype(BF16)
        if own:
            scaled_a[pl.ds(first, size), :] = scaled
            inverse_a[pl.ds(first, size), :] = wide(inverse, 128)
            mid[pl.ds(pl.multiple_of(first + 8, 8), size), :] = block
        return block

    @pl.loop(0, 4)
    def _(step):
        norm_rows(pl.multiple_of(step * 32, 32), 32, True)

    ends = [jnp.int32(0)]
    for record in range(lengths.shape[1]):
        ends.append(ends[-1] + lengths[0, record])

    def start_of(places):
        start = jnp.full(places.shape, BEFORE, jnp.int32)
        for end in ends:
            start = jnp.where(places >= end, end, start)
        return start

    def mask_of(query_places, key_places):
        first = jnp.maximum(start_of(query_places), query_places - LEFT)
        return jnp.where((key_places <= query_places) & (key_places >= first), 0.0, FAR).astype(F32)

    square = (ROWS, ROWS)
    place_rows, place_lanes = offset + iota(square, 0), offset + iota(square, 1)
    mask_main[:, :ROWS] = mask_of(place_rows, place_lanes)
    mask_main[:, ROWS:] = mask_of(place_rows, place_lanes - ROWS)
    mask_next[...] = mask_of(place_lanes + ROWS, place_rows)
    rim_rows = iota((16, EXT), 0)
    rim_places = offset + jnp.where(rim_rows < 8, rim_rows - 8, rim_rows + (ROWS - 8))
    lanes = iota((16, EXT), 1)
    rim_keys = jnp.where(lanes < ROWS, lanes, lanes - 2 * ROWS)
    rim_keys = jnp.where(lanes < 2 * ROWS, rim_keys, lanes - (3 * ROWS + RIM))
    rim_keys = offset + jnp.where(lanes < 2 * ROWS + RIM, rim_keys, lanes - (ROWS + RIM))
    mask_rim[...] = mask_of(rim_places, rim_keys)
    age_rows = offset + iota((ROWS + 8, 128), 0)
    age[...] = age_rows - start_of(age_rows)

    for wave in (0, 1):
        take("0", 0, half, None, wave)
        give("20", 0, half, 0, wave, right)
        take("1", 1, half, None, wave)
        give("21", 1, half, 1, wave, left)
        take("3", 3, half, None, wave)
        give("4", 3, half, None, wave, right)
        give("5", 3, half, None, wave, left)
        for index in (0, 1, 3):
            pass_z(index, (0, 1), wave)
            pass_on(str(index), index, half, None, wave)
    for wave in (0, 1):
        take("4", 4, half, None, wave)
        give("60", 4, half, 0, wave, right)
        take("5", 5, half, None, wave)
        give("61", 5, half, 1, wave, left)
        for part in (0, 1):
            take(f"2{part}", 2, half, part, wave)
            pass_z(2, (part,), wave)
            pass_on(f"2{part}", 2, half, part, wave)
        for index in (4, 5):
            pass_z(index, (0, 1), wave)
            pass_on(str(index), index, half, None, wave)
    for wave in (0, 1):
        for part in (0, 1):
            take(f"6{part}", 6, half, part, wave)
            pass_z(6, (part,), wave)
            pass_on(f"6{part}", 6, half, part, wave)
        for index in (0, 1, 3, 2, 4, 5, 6):
            for part in (0, 1):
                take(f"z{part}{index}", index, 1 - half, part, wave)
                pass_on(f"z{part}{index}", index, 1 - half, part, wave)

    links.arrived("prev", xs.at[pl.ds(ROWS, ROWS), :], earlier)
    links.arrived("next", xs.at[pl.ds(2 * ROWS + RIM, RIM), :], earlier)
    links.arrived("prev2", xs.at[pl.ds(2 * ROWS, RIM), :], earlier)
    links.arrived("cot", cts.at[pl.ds(ROWS, RIM), :], earlier)

    @pl.loop(4, 8)
    def _(step):
        norm_rows(pl.multiple_of(step * 32, 32), 32, False)

    block = norm_rows(2 * ROWS, 2 * RIM, False)
    mid[pl.ds(ROWS + 8, 8), :] = block[RIM : RIM + 8]
    mid[pl.ds(0, 8), :] = xs[pl.ds(2 * ROWS - RIM, RIM), :].astype(F32)[8:]

    for name, index, of_half, part, wave in siblings:
        take("sib" + name, index, of_half, part, wave, 1 - core)

    normed = norm_b[...]
    keys[...] = dot(normed, weights[0]).astype(BF16)
    values[...] = dot(normed, weights[1]).astype(BF16)
    rows = jnp.concatenate(
        [normed[:ROWS], normed[2 * ROWS - RIM : 2 * ROWS], normed[2 * ROWS + RIM :]], axis=0
    )
    projected = dot(rows, weights[2])
    query[...] = projected[:ROWS].astype(BF16)
    query_e[...] = projected[ROWS + 8 : ROWS + 24].astype(BF16)
    links.send("query", query, query_n, earlier)

    def head(index):
        return slice(index * HEAD_DIM, (index + 1) * HEAD_DIM)

    lane = iota(square, 1)
    columns = jnp.zeros(square, F32)
    for h in range(HEADS):
        scores = dot_nt(query[:, head(h)], keys[: 2 * ROWS, head(h)]) * SCALE + mask_main[...]
        top = jnp.max(scores, axis=-1, keepdims=True)
        shifted = jnp.exp(scores - top)
        part = 1.0 / jnp.sum(shifted, axis=-1, keepdims=True)
        share = shifted * part
        probs[h] = share
        context[8 : ROWS + 8, head(h)] = dot(share.astype(BF16), values[: 2 * ROWS, head(h)])
        columns = jnp.where(lane == h, top, columns)
        columns = jnp.where(lane == HEADS + h, part, columns)
        scores = dot_nt(query_e[:, head(h)], keys[:, head(h)]) * SCALE + mask_rim[...]
        shifted = jnp.exp(scores - jnp.max(scores, axis=-1, keepdims=True))
        share = shifted * (1.0 / jnp.sum(shifted, axis=-1, keepdims=True))
        rims = dot(share.astype(BF16), values[:, head(h)])
        context[0:8, head(h)] = rims[:8]
        context[ROWS + 8 :, head(h)] = rims[8:]
    stats[...] = columns.T[:8]
    links.send("stats", stats, stats_n, earlier)

    mid[...] += dot_nt(context[...].astype(BF16), weights[3])

    @pl.loop(0, 3)
    def _(step):
        part_rows = pl.ds(pl.multiple_of(step * 48, 8), 48)
        scaled, inverse = normalize(mid[part_rows, :])
        scaled_c[part_rows, :] = scaled
        inverse_c[part_rows, :] = wide(inverse, 128)
        normed = (scaled * gain_c[...]).astype(BF16).astype(F32)
        for tile in range(WIDTH // 128):
            conv_in[tile, part_rows, :] = normed[:, tile * 128 : (tile + 1) * 128]

    @pl.loop(0, WIDTH // 128)
    def _(tile):
        part_lanes = pl.ds(pl.multiple_of(tile * 128, 128), 128)
        conv = jnp.broadcast_to(bias_ref[:, part_lanes], (ROWS + 8, 128))
        for back_by in range(TAPS):
            term = conv_in[tile, pl.ds(8 - back_by, ROWS + 8), :]
            term = term * taps_ref[TAPS - 1 - back_by : TAPS - back_by, part_lanes]
            conv = conv + jnp.where(age[...] >= back_by, term, 0.0)
        gate = 1.0 / (1.0 + jnp.exp(-conv))
        grad_out = cts[:, part_lanes].astype(F32)[: ROWS + 8]
        grad = grad_out * gate * (1.0 + conv * (1.0 - gate))
        grad_conv[...] = grad
        grad = grad[:ROWS]
        early[tile, 9:10, :] = jnp.sum(grad, axis=0, keepdims=True)
        total = jnp.zeros((ROWS, 128), F32)
        for back_by in range(TAPS):
            tap = TAPS - 1 - back_by
            kept = jnp.where(age[:ROWS, :] >= back_by, grad, 0.0)
            term = kept * conv_in[tile, pl.ds(8 - back_by, ROWS), :]
            early[tile, tap : tap + 1, :] = jnp.sum(term, axis=0, keepdims=True)
            ahead = pl.ds(back_by, ROWS)
            kept = jnp.where(age[ahead, :] >= back_by, grad_conv[ahead, :], 0.0)
            total = total + kept * taps_ref[tap : tap + 1, part_lanes]
        grad_conv_in[:, part_lanes] = total
        term = total * scaled_c[8 : ROWS + 8, part_lanes]
        early[tile, 10:11, :] = jnp.sum(term, axis=0, keepdims=True)
        early[tile, 11:16, :] = jnp.zeros((5, 128), F32)

    def collect(name, me, size, slots):
        for step in range(1, size):
            links.arrived((name, step), slots.at[shift(me, -step, size)], sibling)
        total = slots[0]
        for index in range(1, size):
            total = total + slots[index]
        return total

    early_x[group] = early[group]
    for step in range(1, GROUP):
        other, device = group_peer(step)
        links.send(("ex", step), early.at[other], early_x.at[group], device)

    @pl.loop(0, 4)
    def _(step):
        part_rows = pl.ds(pl.multiple_of(step * 32, 32), 32)
        ext_rows = pl.ds(pl.multiple_of(step * 32 + 8, 8), 32)
        grad, scaled = grad_conv_in[part_rows, :] * gain_c[...], scaled_c[ext_rows, :]
        first = jnp.mean(grad, axis=-1, keepdims=True)
        second = jnp.mean(grad * scaled, axis=-1, keepdims=True)
        result = spread(inverse_c[ext_rows, :]) * (grad - first - scaled * second)
        grad_mid_norm[part_rows, :] = result
        grad_mid_b[part_rows, :] = (cts[part_rows, :].astype(F32) + result).astype(BF16)

    grad_context[...] = dot(grad_mid_b[...], weights[3]).astype(BF16)
    links.send("grad", grad_context, grad_context_n, earlier)
    columns = jnp.zeros(square, F32)
    deltas = []
    for h in range(HEADS):
        term = context[8 : ROWS + 8, head(h)] * grad_context[:, head(h)].astype(F32)
        deltas.append(jnp.sum(term, axis=-1, keepdims=True))
        columns = jnp.where(lane == h, deltas[h], columns)
    delta[...] = columns.T[:8]
    links.send("delta", delta, delta_n, earlier)

    early_y[y] = collect("ex", group, GROUP, early_x)
    for step in range(1, NY):
        links.send(("ey", step), early_y.at[y], early_y.at[y], y_peer(step)[1])

    for h in range(HEADS):
        grad_h = grad_context[:, head(h)]
        share = probs[h]
        grad_probs = dot_nt(grad_h, values[: 2 * ROWS, head(h)])
        grad_scores = (share * (grad_probs - deltas[h]) * SCALE).astype(BF16)
        grad_query[:, head(h)] = dot(grad_scores, keys[: 2 * ROWS, head(h)]).astype(BF16)
        grad_key_f[:, head(h)] = dot_tn(grad_scores[:, :ROWS], query[:, head(h)])
        grad_value_f[:, head(h)] = dot_tn(share[:, :ROWS].astype(BF16), grad_h)

    early_z[z] = collect("ey", y, NY, early_y)
    for step in range(1, NZ):
        links.send(("ez", step), early_z.at[z], early_z.at[z], z_peer(step)[1])
    grad_norm_a[...] = dot_nt(grad_query[...], weights[2])

    links.arrived("query", query_n, earlier)
    links.arrived("stats", stats_n, earlier)
    links.arrived("grad", grad_context_n, earlier)
    links.arrived("delta", delta_n, earlier)
    for h in range(HEADS):
        query_h, grad_h = query_n[:, head(h)], grad_context_n[:, head(h)]
        scores = dot_nt(keys[:ROWS, head(h)], query_h) * SCALE + mask_next[...]
        share = jnp.exp(scores - stats_n[h : h + 1, :]) * stats_n[HEADS + h : HEADS + h + 1, :]
        grad_probs = dot_nt(values[:ROWS, head(h)], grad_h)
        grad_scores = (share * (grad_probs - delta_n[h : h + 1, :]) * SCALE).astype(BF16)
        total = grad_key_f[:, head(h)] + dot(grad_scores, query_h)
        grad_key[:, head(h)] = total.astype(BF16)
        total = grad_value_f[:, head(h)] + dot(share.astype(BF16), grad_h)
        grad_value[:, head(h)] = total.astype(BF16)

    early_all[group] = collect("ez", z, NZ, early_z)
    for step in range(1, GROUP):
        links.send(("ea", step), early_all.at[group], early_all.at[group], group_peer(step)[1])

    grad_norm_a[...] += dot_nt(grad_key[...], weights[0]) + dot_nt(grad_value[...], weights[1])

    product = grad_norm_a[...] * scaled_a[...]
    total = jnp.sum(product, axis=0, keepdims=True)
    for tile in range(WIDTH // 128):
        late_sum[tile : tile + 1, :] = total[:, tile * 128 : (tile + 1) * 128]
    late_x[group] = late_sum[...]
    for step in range(1, GROUP):
        links.send(("lx", step), late_x.at[group], late_x.at[group], group_peer(step)[1])

    @pl.loop(0, 4)
    def _(step):
        part_rows = pl.ds(pl.multiple_of(step * 32, 32), 32)
        grad, scaled = grad_norm_a[part_rows, :] * gain_a[...], scaled_a[part_rows, :]
        first = jnp.mean(grad, axis=-1, keepdims=True)
        second = jnp.mean(grad * scaled, axis=-1, keepdims=True)
        result = spread(inverse_a[part_rows, :]) * (grad - first - scaled * second)
        frames_out[part_rows, :] = grad_mid_norm[part_rows, :] + result

    out_copies = [bring(frames_out, out_frames.at[0])]

    late_y[y] = collect("lx", group, GROUP, late_x)
    for step in range(1, NY):
        links.send(("ly", step), late_y.at[y], late_y.at[y], y_peer(step)[1])

    factor = 1.0 / math.sqrt(NX * 2 * 2 * (NY // 2) * NZ * ROWS)
    for step in range(1, GROUP):
        links.arrived(("ea", step), early_all.at[shift(group, -step, GROUP)], sibling)
    for tile in range(WIDTH // 128):
        part_lanes = slice(tile * 128, (tile + 1) * 128)
        summed = early_all[tile] * factor
        kernel_rows[:, part_lanes] = summed[:TAPS]
        bias_row[:, part_lanes] = summed[9:10]
        conv_row[:, part_lanes] = summed[10:11]
    out_copies.append(bring(kernel_rows, out_kernel))
    out_copies.append(bring(bias_row, out_bias))
    out_copies.append(bring(conv_row, out_conv))

    late_z[z] = collect("ly", y, NY, late_y)
    for step in range(1, NZ):
        links.send(("lz", step), late_z.at[z], late_z.at[z], z_peer(step)[1])
    links.finish()
    summed = collect("lz", z, NZ, late_z) * factor
    for tile in range(WIDTH // 128):
        att_row[:, tile * 128 : (tile + 1) * 128] = summed[tile : tile + 1]
    out_copies.append(bring(att_row, out_att))
    for copy in out_copies:
        copy.wait()


def scratch():
    def buffer(*shape, dtype=F32):
        return pltpu.VMEM(shape, dtype)

    return [
        buffer(EXT, WIDTH, dtype=BF16),
        buffer(CONV, WIDTH, dtype=BF16),
        buffer(4, WIDTH, HEADS_WIDTH, dtype=BF16),
        buffer(HEADS_WIDTH, DEEP, dtype=BF16),
        buffer(1, WIDTH),
        buffer(1, WIDTH),
        buffer(TAPS, WIDTH),
        buffer(1, WIDTH),
        buffer(EXT, WIDTH, dtype=BF16),
        buffer(ROWS, WIDTH),
        buffer(ROWS, 128),
        buffer(EXT, HEADS_WIDTH, dtype=BF16),
        buffer(EXT, HEADS_WIDTH, dtype=BF16),
        buffer(ROWS, HEADS_WIDTH, dtype=BF16),
        buffer(16, HEADS_WIDTH, dtype=BF16),
        buffer(ROWS, HEADS_WIDTH, dtype=BF16),
        buffer(HEADS, ROWS, 2 * ROWS),
        buffer(CONV, HEADS_WIDTH),
        buffer(CONV, WIDTH),
        buffer(CONV, WIDTH),
        buffer(CONV, 128),
        buffer(WIDTH // 128, CONV, 128),
        buffer(ROWS + 8, 128, dtype=jnp.int32),
        buffer(ROWS + 8, 128),
        buffer(ROWS, WIDTH),
        buffer(ROWS, WIDTH),
        buffer(ROWS, WIDTH, dtype=BF16),
        buffer(ROWS, HEADS_WIDTH, dtype=BF16),
        buffer(ROWS, HEADS_WIDTH, dtype=BF16),
        buffer(ROWS, HEADS_WIDTH, dtype=BF16),
        buffer(ROWS, HEADS_WIDTH, dtype=BF16),
        buffer(ROWS, HEADS_WIDTH, dtype=BF16),
        buffer(ROWS, HEADS_WIDTH),
        buffer(ROWS, HEADS_WIDTH),
        buffer(ROWS, WIDTH),
        buffer(ROWS, WIDTH),
        buffer(ROWS, 2 * ROWS),
        buffer(16, EXT),
        buffer(ROWS, ROWS),
        buffer(8, 128),
        buffer(8, 128),
        buffer(8, 128),
        buffer(8, 128),
        buffer(GROUP, 16, 128),
        buffer(GROUP, 16, 128),
        buffer(NY, 16, 128),
        buffer(NZ, 16, 128),
        buffer(GROUP, 16, 128),
        buffer(8, 128),
        buffer(GROUP, 8, 128),
        buffer(NY, 8, 128),
        buffer(NZ, 8, 128),
        buffer(1, WIDTH),
        buffer(1, WIDTH),
        buffer(TAPS, WIDTH),
        buffer(1, WIDTH),
        pltpu.SemaphoreType.DMA((SLOTS,)),
        pltpu.SemaphoreType.DMA((SLOTS,)),
        pltpu.SemaphoreType.DMA((16,)),
    ]


def shards(
    frames, cotangent, lengths, w_query, w_key, w_value, w_output, att_gain, conv_gain, kernel, conv_bias
):
    row = (1, WIDTH)
    anywhere = pl.BlockSpec(memory_space=pl.ANY)
    in_specs = [anywhere] * 11
    in_specs[2] = pl.BlockSpec(memory_space=pltpu.SMEM)
    result = pl.pallas_call(
        block_kernel,
        out_shape=(
            jax.ShapeDtypeStruct(frames.shape, F32),
            jax.ShapeDtypeStruct(row, F32),
            jax.ShapeDtypeStruct(row, F32),
            jax.ShapeDtypeStruct(kernel.shape, F32),
            jax.ShapeDtypeStruct(row, F32),
        ),
        in_specs=in_specs,
        out_specs=(anywhere,) * 5,
        scratch_shapes=scratch(),
        compiler_params=pltpu.CompilerParams(
            collective_id=0, has_side_effects=True, vmem_limit_bytes=48 << 20
        ),
        cost_estimate=pl.CostEstimate(
            flops=3 << 30, bytes_accessed=4 << 20, transcendentals=1 << 20
        ),
    )(
        frames, cotangent, lengths, w_query, w_key, w_value, w_output,
        att_gain.reshape(row), conv_gain.reshape(row), kernel, conv_bias.reshape(row),
    )
    grad_frames, grad_att, grad_conv, grad_kernel, grad_bias = result
    return (
        grad_frames,
        grad_att.reshape(WIDTH),
        grad_conv.reshape(WIDTH),
        grad_kernel,
        grad_bias.reshape(WIDTH),
    )


def solution(mesh):
    return jax.shard_map(
        shards,
        mesh=mesh,
        in_specs=(
            P("dp", "ctx", None),
            P("dp", "ctx", None),
            P("dp", None),
            P("dp", None),
            P("dp", None),
            P("dp", None),
            P(None, "dp"),
            P(),
            P(),
            P(),
            P(),
        ),
        out_specs=(P("dp", "ctx", None), P(), P(), P(), P()),
        check_vma=False,
    )
```

time: 340 us -> 91.7 us (0.27)
  waiting for transfers between devices: 166 us -> 0 us
  blocking collectives: 102 us -> 0 us
  Pallas kernels: 0 us -> 81.6 us
  matrix products: 20.7 us -> 0 us
  starting transfers between devices: 16.5 us -> 0 us
  between operations: 14.5 us -> 0.73 us
  other arithmetic: 8.58 us -> 0 us
    all_gather x4 -> x0, waiting for transfers between devices: 146 us -> none  [the longest x1 42.3 us: shards(): lax.all_gather(w_value, 'dp', axis=0, tiled=True)]
    psum x1 -> x0, blocking collectives: 102 us -> none  [shards(): lax.psum((grad_kernel, grad_bias, grad_conv_gain, grad_att_gain), ('dp',...]
    pallas_call x0 -> x1, Pallas kernels: none -> 81.6 us  [shards(): pl.pallas_call(block_kernel, out_shape=(jax.ShapeDtypeStruct(frames.shape...]
    dot_general x13 -> x0, matrix products: 19.6 us -> none  [the longest x1 4.78 us: shards(): jnp.einsum('shqk,skhd->sqhd', grad_scores, windows(keys_ext, first, block...]
    ppermute x6 -> x0, waiting for transfers between devices: 17.4 us -> none  [shifted_2(): return lax.ppermute(block, axis, route)]
    ppermute x6 -> x0, starting transfers between devices: 16.3 us -> none  [shifted_2(): return lax.ppermute(block, axis, route)]
    unnamed x82 -> x26, local copies, waits for them, and re-layouts: 5.7 us -> 9.02 us
  transfers between devices with their start and end apart: 10 -> 0, of which waited for: 7 -> 0; matrix products, arithmetic and copies ran while one was open for 3% -> 0% of each run, Pallas kernels for 0% -> 0%
where the time goes in v1:
time: 91.7 us; the launch traced here: 91.3 us
  Pallas kernels  81.6 us (89%)
  local copies, waits for them, and re-layouts  9.02 us (10%)
    pallas_call x1, Pallas kernels, shards(): pl.pallas_call(block_kernel, out_shape=(jax.ShapeDtypeStruct(frames.shape...  81.6 us
    unnamed x26, local copies, waits for them, and re-layouts  9.02 us

profile of v1, /device:TPU:1, one launch (start us, length us, event | category | flops | bytes accessed | tf_op | source)
XLA Modules:
  0.0 91.3 jit_solution(3686600135911659282)
XLA Ops:
  0.6 0.0 copy-start.9
  0.6 0.0 copy-start.2
  0.7 0.0 copy-start.3
  0.7 0.0 copy-start.4
  0.7 1.0 %copy.16.w_output = bf16[512,64]{1,0:T(8,128)(2,1)S(1)} copy(bf16[512,64]{0,1:T(8,128)(2,1)} %param.17) | data formatting | bytes 131072 | tf_op args[6]
  1.7 0.0 copy-done.9
  1.7 0.0 copy-done.2
  1.7 0.0 copy-done.3
  1.7 0.0 copy-done.4
  1.7 0.0 copy-start
  1.7 0.9 %copy-done = bf16[1,128,1024]{2,1,0:T(8,128)(2,1)S(1)} copy-done((bf16[1,128,1024]{2,1,0:T(8,128)(2,1)S(1)}, bf16[1,128,1024]{2,1,0:T(8,128)(2,1)}, u32[]{:S(2)}) %copy-start) | copy-done | bytes 262168
  2.7 0.0 copy-start.1
  2.7 0.9 %copy-done.1 = bf16[1,128,1024]{2,1,0:T(8,128)(2,1)S(1)} copy-done((bf16[1,128,1024]{2,1,0:T(8,128)(2,1)S(1)}, bf16[1,128,1024]{2,1,0:T(8,128)(2,1)}, u32[]{:S(2)}) %copy-start.1) | copy-done | bytes 262168
  3.6 0.0 copy-start.5
  3.6 0.8 copy-done.5
  4.5 0.7 copy-done.6
  5.2 0.7 copy-done.7
  5.8 0.7 copy-done.8
  6.5 81.6 %shard_map.146 = (f32[1,128,1024]{2,1,0:T(8,128)S(1)}, f32[1,1024]{1,0:T(1,128)S(1)}, f32[1,1024]{1,0:T(1,128)S(1)}, f32[9,1024]{1,0:T(8,128)S(1)}, f32[1,1024]{1,0:T(1,128)S(1)}) custom-call(bf16[1,128,1024]{2,1,0:T(8,128)(2,1)S(1)} %copy-done, bf16[1,128,1024]{2,1,0:T(8,128)(2,1)S(1)} %copy-done.1, s32[1,4]{1,0:T(1,128)S(1)} %copy-done.9, ...), custom_call_target="tpu_custom_call" | custom-call | flops 3221225472 | bytes 4194304 | tf_op jit(solution)/shard_map/pallas_call | solution.py:593
  88.1 0.8 copy.22
  88.9 0.6 copy.23
  89.5 0.6 copy.24
  90.1 0.6 copy.25
  90.8 0.6 copy.26
  (3 shorter events, 0.0 us)
Async XLA Ops:
  0.6 1.1 %copy-start.9 = (s32[1,4]{1,0:T(1,128)S(1)}, s32[1,4]{1,0:T(1,128)}, u32[]{:S(2)}) copy-start(s32[1,4]{1,0:T(1,128)} %lengths.1) | copy-start | bytes 52
  0.6 1.1 %copy-start.2 = (bf16[64,512]{1,0:T(8,128)(2,1)S(1)}, bf16[64,512]{1,0:T(8,128)(2,1)}, u32[]{:S(2)}) copy-start(bf16[64,512]{1,0:T(8,128)(2,1)} %w_query.1) | copy-start | bytes 196612
  0.7 1.1 %copy-start.3 = (bf16[64,512]{1,0:T(8,128)(2,1)S(1)}, bf16[64,512]{1,0:T(8,128)(2,1)}, u32[]{:S(2)}) copy-start(bf16[64,512]{1,0:T(8,128)(2,1)} %w_key.1) | copy-start | bytes 196612
  0.7 1.1 %copy-start.4 = (bf16[64,512]{1,0:T(8,128)(2,1)S(1)}, bf16[64,512]{1,0:T(8,128)(2,1)}, u32[]{:S(2)}) copy-start(bf16[64,512]{1,0:T(8,128)(2,1)} %w_value.1) | copy-start | bytes 196612
  1.7 1.0 %copy-start = (bf16[1,128,1024]{2,1,0:T(8,128)(2,1)S(1)}, bf16[1,128,1024]{2,1,0:T(8,128)(2,1)}, u32[]{:S(2)}) copy-start(bf16[1,128,1024]{2,1,0:T(8,128)(2,1)} %frames.1) | copy-start | bytes 786436
  2.7 0.9 %copy-start.1 = (bf16[1,128,1024]{2,1,0:T(8,128)(2,1)S(1)}, bf16[1,128,1024]{2,1,0:T(8,128)(2,1)}, u32[]{:S(2)}) copy-start(bf16[1,128,1024]{2,1,0:T(8,128)(2,1)} %cotangent.1) | copy-start | bytes 786436
  3.6 0.8 copy-start.5
  4.5 0.7 copy-start.6
  5.2 0.7 copy-start.7
  5.8 0.7 copy-start.8

commit v2 on v1

--- a/solution.py
+++ b/solution.py
@@ -94,14 +94,14 @@
 
 def block_kernel(
     frames, cotangent, lengths, w_query, w_key, w_value, w_output, att_gain, conv_gain, kernel, bias,
-    out_frames, out_att, out_conv, out_kernel, out_bias,
-    xs, cts, weights, w_in, gain_a, gain_c, taps_ref, bias_ref,
+    out_frames, out_sums,
+    xs, cts, weights, gain_a, gain_c, taps_ref, bias_ref,
     norm_b, scaled_a, inverse_a, keys, values, query, query_e, query_n, probs, context, mid,
     scaled_c, inverse_c, conv_in, age, grad_conv, grad_conv_in, grad_mid_norm, grad_mid_b,
-    grad_context, grad_context_n, grad_query, grad_key, grad_value, grad_key_f, grad_value_f, grad_norm_a,
+    grad_context, grad_context_n, grad_query, grad_key, grad_value, grad_norm_a,
     frames_out, mask_main, mask_rim, mask_next, stats, stats_n, delta, delta_n,
     early, early_x, early_y, early_z, early_all, late_sum, late_x, late_y, late_z,
-    att_row, conv_row, kernel_rows, bias_row,
+    sums,
     send_sems, recv_sems, local_sems,
 ):
     dp, ctx = lax.axis_index("dp"), lax.axis_index("ctx")
@@ -150,10 +150,9 @@
         return copy
 
     own_rows = pl.ds(pl.multiple_of(dp * DEEP, DEEP), DEEP)
-    got_output = bring(w_output, w_in)
     got_weights = [
         bring(source, weights.at[index, own_rows, :])
-        for index, source in ((0, w_key), (1, w_value), (2, w_query))
+        for index, source in ((0, w_key), (1, w_value), (2, w_query), (3, w_output))
     ]
     got_frames = bring(frames.at[0], xs.at[pl.ds(0, ROWS), :])
     got_rest = [
@@ -171,16 +170,9 @@
     peers += [later, earlier, later_2, frames_at(-2)]
     for peer in peers:
         pl.semaphore_signal(barrier, inc=1, device_id=peer, device_id_type=MESH)
-    got_output.wait()
-    weights[3, own_rows, :] = w_in[...].astype(F32).T.astype(BF16)
     for copy in got_weights:
         copy.wait()
     pl.semaphore_wait(barrier, len(peers))
-
-    links.send("prev", frames.at[0], xs.at[pl.ds(ROWS, ROWS), :], later)
-    links.send("next", frames.at[0, pl.ds(0, RIM), :], xs.at[pl.ds(2 * ROWS + RIM, RIM), :], earlier)
-    links.send("prev2", frames.at[0, pl.ds(ROWS - RIM, RIM), :], xs.at[pl.ds(2 * ROWS, RIM), :], later_2)
-    links.send("cot", cotangent.at[0, pl.ds(0, RIM), :], cts.at[pl.ds(ROWS, RIM), :], earlier)
 
     half = lax.rem(z, 2)
 
@@ -223,6 +215,11 @@
         give("3", None, half, None, wave, below)
         pass_on("own", None, None, None, wave)
 
+    links.send("prev", frames.at[0], xs.at[pl.ds(ROWS, ROWS), :], later)
+    links.send("next", frames.at[0, pl.ds(0, RIM), :], xs.at[pl.ds(2 * ROWS + RIM, RIM), :], earlier)
+    links.send("prev2", frames.at[0, pl.ds(ROWS - RIM, RIM), :], xs.at[pl.ds(2 * ROWS, RIM), :], later_2)
+    links.send("cot", cotangent.at[0, pl.ds(0, RIM), :], cts.at[pl.ds(ROWS, RIM), :], earlier)
+
     got_frames.wait()
     for copy in got_rest:
         copy.wait()
@@ -231,8 +228,9 @@
         block = xs[pl.ds(first, size), :].astype(F32)
         scaled, inverse = normalize(block)
         norm_b[pl.ds(first, size), :] = (scaled * gain_a[...]).astype(BF16)
+        if own is not None:
+            scaled_a[pl.ds(first, size), :] = scaled
         if own:
-            scaled_a[pl.ds(first, size), :] = scaled
             inverse_a[pl.ds(first, size), :] = wide(inverse, 128)
             mid[pl.ds(pl.multiple_of(first + 8, 8), size), :] = block
         return block
@@ -312,7 +310,7 @@
     def _(step):
         norm_rows(pl.multiple_of(step * 32, 32), 32, False)
 
-    block = norm_rows(2 * ROWS, 2 * RIM, False)
+    block = norm_rows(2 * ROWS, 2 * RIM, None)
     mid[pl.ds(ROWS + 8, 8), :] = block[RIM : RIM + 8]
     mid[pl.ds(0, 8), :] = xs[pl.ds(2 * ROWS - RIM, RIM), :].astype(F32)[8:]
 
@@ -429,23 +427,35 @@
     delta[...] = columns.T[:8]
     links.send("delta", delta, delta_n, earlier)
 
-    early_y[y] = collect("ex", group, GROUP, early_x)
-    for step in range(1, NY):
-        links.send(("ey", step), early_y.at[y], early_y.at[y], y_peer(step)[1])
-
     for h in range(HEADS):
         grad_h = grad_context[:, head(h)]
         share = probs[h]
         grad_probs = dot_nt(grad_h, values[: 2 * ROWS, head(h)])
         grad_scores = (share * (grad_probs - deltas[h]) * SCALE).astype(BF16)
         grad_query[:, head(h)] = dot(grad_scores, keys[: 2 * ROWS, head(h)]).astype(BF16)
-        grad_key_f[:, head(h)] = dot_tn(grad_scores[:, :ROWS], query[:, head(h)])
-        grad_value_f[:, head(h)] = dot_tn(share[:, :ROWS].astype(BF16), grad_h)
-
+        grad_key[:, head(h)] = dot_tn(grad_scores, query[:, head(h)]).astype(BF16)
+        grad_value[:, head(h)] = dot_tn(share.astype(BF16), grad_h).astype(BF16)
+
+    parts = dot_nt(grad_key[...], weights[0]) + dot_nt(grad_value[...], weights[1])
+    own_part = parts[:ROWS] + dot_nt(grad_query[...], weights[2])
+    grad_norm_a[...] = own_part
+    product = own_part * scaled_a[:ROWS] + parts[ROWS:] * scaled_a[ROWS:]
+    total = jnp.sum(product, axis=0, keepdims=True)
+    for tile in range(WIDTH // 128):
+        late_sum[tile : tile + 1, :] = total[:, tile * 128 : (tile + 1) * 128]
+    late_x[group] = late_sum[...]
+    for step in range(1, GROUP):
+        links.send(("lx", step), late_x.at[group], late_x.at[group], group_peer(step)[1])
+
+    early_y[y] = collect("ex", group, GROUP, early_x)
+    for step in range(1, NY):
+        links.send(("ey", step), early_y.at[y], early_y.at[y], y_peer(step)[1])
+    late_y[y] = collect("lx", group, GROUP, late_x)
+    for step in range(1, NY):
+        links.send(("ly", step), late_y.at[y], late_y.at[y], y_peer(step)[1])
     early_z[z] = collect("ey", y, NY, early_y)
     for step in range(1, NZ):
         links.send(("ez", step), early_z.at[z], early_z.at[z], z_peer(step)[1])
-    grad_norm_a[...] = dot_nt(grad_query[...], weights[2])
 
     links.arrived("query", query_n, earlier)
     links.arrived("stats", stats_n, earlier)
@@ -457,24 +467,17 @@
         share = jnp.exp(scores - stats_n[h : h + 1, :]) * stats_n[HEADS + h : HEADS + h + 1, :]
         grad_probs = dot_nt(values[:ROWS, head(h)], grad_h)
         grad_scores = (share * (grad_probs - delta_n[h : h + 1, :]) * SCALE).astype(BF16)
-        total = grad_key_f[:, head(h)] + dot(grad_scores, query_h)
-        grad_key[:, head(h)] = total.astype(BF16)
-        total = grad_value_f[:, head(h)] + dot(share.astype(BF16), grad_h)
-        grad_value[:, head(h)] = total.astype(BF16)
-
+        grad_key[:ROWS, head(h)] = dot(grad_scores, query_h).astype(BF16)
+        grad_value[:ROWS, head(h)] = dot(share.astype(BF16), grad_h).astype(BF16)
+
+    late_z[z] = collect("ly", y, NY, late_y)
+    for step in range(1, NZ):
+        links.send(("lz", step), late_z.at[z], late_z.at[z], z_peer(step)[1])
     early_all[group] = collect("ez", z, NZ, early_z)
     for step in range(1, GROUP):
         links.send(("ea", step), early_all.at[group], early_all.at[group], group_peer(step)[1])
 
-    grad_norm_a[...] += dot_nt(grad_key[...], weights[0]) + dot_nt(grad_value[...], weights[1])
-
-    product = grad_norm_a[...] * scaled_a[...]
-    total = jnp.sum(product, axis=0, keepdims=True)
-    for tile in range(WIDTH // 128):
-        late_sum[tile : tile + 1, :] = total[:, tile * 128 : (tile + 1) * 128]
-    late_x[group] = late_sum[...]
-    for step in range(1, GROUP):
-        links.send(("lx", step), late_x.at[group], late_x.at[group], group_peer(step)[1])
+    grad_norm_a[...] += dot_nt(grad_key[:ROWS], weights[0]) + dot_nt(grad_value[:ROWS], weights[1])
 
     @pl.loop(0, 4)
     def _(step):
@@ -485,35 +488,30 @@
         result = spread(inverse_a[part_rows, :]) * (grad - first - scaled * second)
         frames_out[part_rows, :] = grad_mid_norm[part_rows, :] + result
 
-    out_copies = [bring(frames_out, out_frames.at[0])]
-
-    late_y[y] = collect("lx", group, GROUP, late_x)
-    for step in range(1, NY):
-        links.send(("ly", step), late_y.at[y], late_y.at[y], y_peer(step)[1])
+    out_copy = bring(frames_out, out_frames.at[0])
+    links.finish()
 
     factor = 1.0 / math.sqrt(NX * 2 * 2 * (NY // 2) * NZ * ROWS)
     for step in range(1, GROUP):
         links.arrived(("ea", step), early_all.at[shift(group, -step, GROUP)], sibling)
     for tile in range(WIDTH // 128):
-        part_lanes = slice(tile * 128, (tile + 1) * 128)
-        summed = early_all[tile] * factor
-        kernel_rows[:, part_lanes] = summed[:TAPS]
-        bias_row[:, part_lanes] = summed[9:10]
-        conv_row[:, part_lanes] = summed[10:11]
-    out_copies.append(bring(kernel_rows, out_kernel))
-    out_copies.append(bring(bias_row, out_bias))
-    out_copies.append(bring(conv_row, out_conv))
-
-    late_z[z] = collect("ly", y, NY, late_y)
-    for step in range(1, NZ):
-        links.send(("lz", step), late_z.at[z], late_z.at[z], z_peer(step)[1])
-    links.finish()
+        sums[:, tile * 128 : (tile + 1) * 128] = early_all[tile] * factor
     summed = collect("lz", z, NZ, late_z) * factor
     for tile in range(WIDTH // 128):
-        att_row[:, tile * 128 : (tile + 1) * 128] = summed[tile : tile + 1]
-    out_copies.append(bring(att_row, out_att))
-    for copy in out_copies:
-        copy.wait()
+        sums[11:12, tile * 128 : (tile + 1) * 128] = summed[tile : tile + 1]
+    bring(sums, out_sums).wait()
+    out_copy.wait()
+
+
+def finish_kernel(frames_in, sums, out_frames, out_att, out_conv, out_kernel, out_bias):
+    out_frames[...] = frames_in[...]
+
+    @pl.when(pl.program_id(0) == 0)
+    def _():
+        out_kernel[...] = sums[:TAPS]
+        out_bias[...] = sums[9:10]
+        out_conv[...] = sums[10:11]
+        out_att[...] = sums[11:12]
 
 
 def scratch():
@@ -524,13 +522,12 @@
         buffer(EXT, WIDTH, dtype=BF16),
         buffer(CONV, WIDTH, dtype=BF16),
         buffer(4, WIDTH, HEADS_WIDTH, dtype=BF16),
-        buffer(HEADS_WIDTH, DEEP, dtype=BF16),
         buffer(1, WIDTH),
         buffer(1, WIDTH),
         buffer(TAPS, WIDTH),
         buffer(1, WIDTH),
         buffer(EXT, WIDTH, dtype=BF16),
-        buffer(ROWS, WIDTH),
+        buffer(2 * ROWS, WIDTH),
         buffer(ROWS, 128),
         buffer(EXT, HEADS_WIDTH, dtype=BF16),
         buffer(EXT, HEADS_WIDTH, dtype=BF16),
@@ -551,10 +548,8 @@
         buffer(ROWS, HEADS_WIDTH, dtype=BF16),
         buffer(ROWS, HEADS_WIDTH, dtype=BF16),
         buffer(ROWS, HEADS_WIDTH, dtype=BF16),
-        buffer(ROWS, HEADS_WIDTH, dtype=BF16),
-        buffer(ROWS, HEADS_WIDTH, dtype=BF16),
-        buffer(ROWS, HEADS_WIDTH),
-        buffer(ROWS, HEADS_WIDTH),
+        buffer(2 * ROWS, HEADS_WIDTH, dtype=BF16),
+        buffer(2 * ROWS, HEADS_WIDTH, dtype=BF16),
         buffer(ROWS, WIDTH),
         buffer(ROWS, WIDTH),
         buffer(ROWS, 2 * ROWS),
@@ -573,10 +568,7 @@
         buffer(GROUP, 8, 128),
         buffer(NY, 8, 128),
         buffer(NZ, 8, 128),
-        buffer(1, WIDTH),
-        buffer(1, WIDTH),
-        buffer(TAPS, WIDTH),
-        buffer(1, WIDTH),
+        buffer(16, WIDTH),
         pltpu.SemaphoreType.DMA((SLOTS,)),
         pltpu.SemaphoreType.DMA((SLOTS,)),
         pltpu.SemaphoreType.DMA((16,)),
@@ -590,8 +582,34 @@
     anywhere = pl.BlockSpec(memory_space=pl.ANY)
     in_specs = [anywhere] * 11
     in_specs[2] = pl.BlockSpec(memory_space=pltpu.SMEM)
-    result = pl.pallas_call(
+    frames_sum, sums = pl.pallas_call(
         block_kernel,
+        out_shape=(
+            jax.ShapeDtypeStruct(frames.shape, F32),
+            jax.ShapeDtypeStruct((16, WIDTH), F32),
+        ),
+        in_specs=in_specs,
+        out_specs=(anywhere,) * 2,
+        scratch_shapes=scratch(),
+        compiler_params=pltpu.CompilerParams(
+            collective_id=0, has_side_effects=True, vmem_limit_bytes=63 << 20
+        ),
+        cost_estimate=pl.CostEstimate(
+            flops=3 << 30, bytes_accessed=4 << 20, transcendentals=1 << 20
+        ),
+    )(
+        frames, cotangent, lengths, w_query, w_key, w_value, w_output.T,
+        att_gain.reshape(row), conv_gain.reshape(row), kernel, conv_bias.reshape(row),
+    )
+    steps = 2
+    moving = pl.BlockSpec((1, ROWS // steps, WIDTH), lambda step: (0, step, 0))
+
+    def fixed(rows):
+        return pl.BlockSpec((rows, WIDTH), lambda step: (0, 0))
+
+    grad_frames, grad_att, grad_conv, grad_kernel, grad_bias = pl.pallas_call(
+        finish_kernel,
+        grid=(steps,),
         out_shape=(
             jax.ShapeDtypeStruct(frames.shape, F32),
             jax.ShapeDtypeStruct(row, F32),
@@ -599,20 +617,10 @@
             jax.ShapeDtypeStruct(kernel.shape, F32),
             jax.ShapeDtypeStruct(row, F32),
         ),
-        in_specs=in_specs,
-        out_specs=(anywhere,) * 5,
-        scratch_shapes=scratch(),
-        compiler_params=pltpu.CompilerParams(
-            collective_id=0, has_side_effects=True, vmem_limit_bytes=48 << 20
-        ),
-        cost_estimate=pl.CostEstimate(
-            flops=3 << 30, bytes_accessed=4 << 20, transcendentals=1 << 20
-        ),
-    )(
-        frames, cotangent, lengths, w_query, w_key, w_value, w_output,
-        att_gain.reshape(row), conv_gain.reshape(row), kernel, conv_bias.reshape(row),
-    )
-    grad_frames, grad_att, grad_conv, grad_kernel, grad_bias = result
+        in_specs=[moving, fixed(16)],
+        out_specs=(moving, fixed(1), fixed(1), fixed(TAPS), fixed(1)),
+        compiler_params=pltpu.CompilerParams(vmem_limit_bytes=63 << 20),
+    )(frames_sum, sums)
     return (
         grad_frames,
         grad_att.reshape(WIDTH),

time: 91.7 us -> 71 us (0.77)
  Pallas kernels: 81.6 us -> 70.2 us
  local copies, waits for them, and re-layouts: 9.02 us -> 0 us
    pallas_call x1, Pallas kernels: 81.6 us -> 68.3 us  [shards(): pl.pallas_call(block_kernel, out_shape=(jax.ShapeDtypeStruct(frames.shape...]
    unnamed x26 -> x0, local copies, waits for them, and re-layouts: 9.02 us -> none
    pallas_call x0 -> x1, Pallas kernels: none -> 1.83 us  [shards(): pl.pallas_call(finish_kernel, grid=(steps,), out_shape=(jax.ShapeDtypeStr...]
where the time goes in v2:
time: 71 us; the launch traced here: 70.8 us
  Pallas kernels  70.2 us (99%)
    pallas_call x1, Pallas kernels, shards(): pl.pallas_call(block_kernel, out_shape=(jax.ShapeDtypeStruct(frames.shape...  68.3 us
    pallas_call x1, Pallas kernels, shards(): pl.pallas_call(finish_kernel, grid=(steps,), out_shape=(jax.ShapeDtypeStr...  1.83 us

profile of v2, /device:TPU:1, one launch (start us, length us, event | category | flops | bytes accessed | tf_op | source)
XLA Modules:
  0.0 70.8 jit_solution(14917148946647933431)
XLA Ops:
  0.6 68.3 %shard_map.146 = (f32[1,128,1024]{2,1,0:T(8,128)}, f32[16,1024]{1,0:T(8,128)}) custom-call(bf16[1,128,1024]{2,1,0:T(8,128)(2,1)} %frames.1, bf16[1,128,1024]{2,1,0:T(8,128)(2,1)} %cotangent.1, s32[1,4]{1,0:T(1,128)} %lengths.1, bf16[64,512]{1,0:T(8,128)(2,1)} %w_query.1, bf16[64,512]{1,0:T(8,128)(2,1)} %w_key.1, bf16[64,512]{1,0:T(8,128)(2,1)} %w_value.1, ...), custom_call_target="tpu_custom_call" | custom-call | flops 3221225472 | bytes 4194304 | tf_op jit(solution)/shard_map/pallas_call | solution.py:585
  69.0 1.8 %shard_map.147 = (f32[1,128,1024]{2,1,0:T(8,128)}, f32[1,1024]{1,0:T(1,128)}, f32[1,1024]{1,0:T(1,128)}, f32[9,1024]{1,0:T(8,128)}, f32[1,1024]{1,0:T(1,128)}) custom-call(f32[1,128,1024]{2,1,0:T(8,128)} %get-tuple-element.12.frames_in, f32[16,1024]{1,0:T(8,128)} %get-tuple-element.13.sums), custom_call_target="tpu_custom_call" | custom-call | tf_op jit(solution)/shard_map/pallas_call | solution.py:610

commit v3 on v2

--- a/solution.py
+++ b/solution.py
@@ -29,7 +29,10 @@
 F32 = jnp.float32
 BF16 = jnp.bfloat16
 
-SHARDS = ((-1, 0), (1, 0), (2, 0), (0, 1), (-1, 1), (1, 1), (2, 1))
+SHARDS = ((-1, 0), (1, 0), (2, 0), (0, 1), (-1, 1), (1, 1), (2, 1), (0, 0))
+DIRECT_SHARDS, FAR_SHARDS, OWN = (4, 5, 0, 1), (6, 2), 7
+LATER, HALVED, FORWARD = (0, 1, 3), (4, 5, 6, 2), ((4, 0), (5, 0), (6, 0))
+RELAYED = {0: (2, 0), 1: (2, 1), 4: (6, 0), 5: (6, 1)}
 
 
 class Links:
@@ -96,7 +99,7 @@
     frames, cotangent, lengths, w_query, w_key, w_value, w_output, att_gain, conv_gain, kernel, bias,
     out_frames, out_sums,
     xs, cts, weights, gain_a, gain_c, taps_ref, bias_ref,
-    norm_b, scaled_a, inverse_a, keys, values, query, query_e, query_n, probs, context, mid,
+    norm_b, scaled_a, inverse_a, keys, values, query, query_e, query_n, probs, probs_rim, context, mid,
     scaled_c, inverse_c, conv_in, age, grad_conv, grad_conv_in, grad_mid_norm, grad_mid_b,
     grad_context, grad_context_n, grad_query, grad_key, grad_value, grad_norm_a,
     frames_out, mask_main, mask_rim, mask_next, stats, stats_n, delta, delta_n,
@@ -105,40 +108,57 @@
     send_sems, recv_sems, local_sems,
 ):
     dp, ctx = lax.axis_index("dp"), lax.axis_index("ctx")
-    core = lax.rem(dp, 2)
-    x = lax.rem(lax.div(dp, 2), NX)
-    y_lo = lax.div(dp, 2 * NX)
+    pair = lax.div(dp, 2)
+    core = dp - 2 * pair
+    y_lo = lax.div(pair, NX)
+    x = pair - NX * y_lo
     z = lax.div(ctx, NY // 2)
-    y = lax.rem(ctx, NY // 2) * 2 + y_lo
+    y_hi = ctx - (NY // 2) * z
+    y = 2 * y_hi + y_lo
     offset = ctx * ROWS
     group = x * 2 + core
 
-    def at(px, py, pz, pc):
-        return ((lax.rem(py, 2) * NX + px) * 2 + pc, pz * (NY // 2) + lax.div(py, 2))
-
-    def shift(value, step, size):
-        return lax.rem(value + (step + size), size)
+    def wrap(value, step, size):
+        moved = value + step
+        if isinstance(step, int) and step < 0:
+            return jnp.where(moved < 0, moved + size, moved)
+        return jnp.where(moved >= size, moved - size, moved)
+
+    def flip(bit, change):
+        return 1 - bit if change else bit
+
+    def at(px, p_hi, p_lo, pz, pc):
+        return ((p_lo * NX + px) * 2 + pc, pz * (NY // 2) + p_hi)
 
     def frames_at(step):
-        return (dp, shift(ctx, step, 4 * NZ))
-
-    sibling = (dp + 1 - 2 * core, ctx)
-    right, left = at(shift(x, 1, NX), y, z, core), at(shift(x, -1, NX), y, z, core)
-    above, below = at(x, shift(y, 1, NY), z, core), at(x, shift(y, -1, NY), z, core)
-    front, back = at(x, y, shift(z, 1, NZ), core), at(x, y, shift(z, -1, NZ), core)
+        return (dp, wrap(ctx, step, NZ * NY // 2))
+
+    sibling = at(x, y_hi, y_lo, z, 1 - core)
+    y_below = jnp.where(y_hi + y_lo == 0, NY // 2 - 1, y_hi + y_lo - 1)
+    right, left = at(wrap(x, 1, NX), y_hi, y_lo, z, core), at(wrap(x, -1, NX), y_hi, y_lo, z, core)
+    y_above = wrap(y_hi, y_lo, NY // 2)
+    corners_above = [at(wrap(x, step, NX), y_above, 1 - y_lo, z, core) for step in (-1, 1)]
+    corners_below = [at(wrap(x, step, NX), y_below, 1 - y_lo, z, core) for step in (-1, 1)]
+    below = at(x, y_below, 1 - y_lo, z, core)
+    front, back = at(x, y_hi, y_lo, wrap(z, 1, NZ), core), at(x, y_hi, y_lo, wrap(z, -1, NZ), core)
     later, earlier, later_2 = frames_at(1), frames_at(-1), frames_at(2)
 
-    def group_peer(step):
-        other = shift(group, step, GROUP)
-        return other, at(lax.div(other, 2), y, z, lax.rem(other, 2))
-
-    def y_peer(step):
-        other = shift(y, step, NY)
-        return other, at(x, other, z, core)
-
-    def z_peer(step):
-        other = shift(z, step, NZ)
-        return other, at(x, y, other, core)
+    group_steps, y_steps, z_steps = [], [], []
+    for step in (2, 1, -1, 0):
+        for change in (1, 0):
+            if (step, change) != (0, 0):
+                to, of = wrap(x, step, NX), wrap(x, -step, NX)
+                pc = flip(core, change)
+                group_steps.append(((step, change), to * 2 + pc, at(to, y_hi, y_lo, z, pc), of * 2 + pc))
+    for step in (2, -1, 1, 0):
+        for change in (1, 0):
+            if (step, change) != (0, 0):
+                to, of = wrap(y_hi, step, NY // 2), wrap(y_hi, -step, NY // 2)
+                lo = flip(y_lo, change)
+                y_steps.append(((step, change), to * 2 + lo, at(x, to, lo, z, core), of * 2 + lo))
+    for step in (4, 3, -3, 2, -2, 1, -1):
+        to, of = wrap(z, step, NZ), wrap(z, -step, NZ)
+        z_steps.append((step, to, at(x, y_hi, y_lo, to, core), of))
 
     links = Links(send_sems, recv_sems)
     local = []
@@ -149,10 +169,17 @@
         local.append(copy)
         return copy
 
+    barrier = pltpu.get_barrier_semaphore()
+    peers = [step[2] for step in group_steps + y_steps + z_steps]
+    peers += [later, earlier, later_2, frames_at(-2)]
+    peers += corners_above + corners_below
+    for peer in peers:
+        pl.semaphore_signal(barrier, inc=1, device_id=peer, device_id_type=MESH)
+
     own_rows = pl.ds(pl.multiple_of(dp * DEEP, DEEP), DEEP)
     got_weights = [
         bring(source, weights.at[index, own_rows, :])
-        for index, source in ((0, w_key), (1, w_value), (2, w_query), (3, w_output))
+        for index, source in ((0, w_key), (1, w_query), (2, w_value), (3, w_output))
     ]
     got_frames = bring(frames.at[0], xs.at[pl.ds(0, ROWS), :])
     got_rest = [
@@ -163,25 +190,15 @@
         bring(bias, bias_ref),
     ]
 
-    barrier = pltpu.get_barrier_semaphore()
-    peers = [group_peer(step)[1] for step in range(1, GROUP)]
-    peers += [y_peer(step)[1] for step in range(1, NY)]
-    peers += [z_peer(step)[1] for step in range(1, NZ)]
-    peers += [later, earlier, later_2, frames_at(-2)]
-    for peer in peers:
-        pl.semaphore_signal(barrier, inc=1, device_id=peer, device_id_type=MESH)
     for copy in got_weights:
         copy.wait()
     pl.semaphore_wait(barrier, len(peers))
 
-    half = lax.rem(z, 2)
+    half = z - 2 * lax.div(z, 2)
 
     def shard(index, of_core):
-        if index is None:
-            return (y_lo * NX + x) * 2 + of_core
         step, other = SHARDS[index]
-        side = 1 - y_lo if other else y_lo
-        return (side * NX + shift(x, step, NX)) * 2 + of_core
+        return (flip(y_lo, other) * NX + wrap(x, step, NX)) * 2 + of_core
 
     def piece(index, of_half, part, wave, of_core):
         first, size = shard(index, of_core) * DEEP, DEEP
@@ -205,15 +222,15 @@
         give("sib" + name, index, of_half, part, wave, sibling)
         siblings.append((name, index, of_half, part, wave))
 
-    def pass_z(index, parts, wave):
-        for part in parts:
-            give(f"z{part}{index}", index, half, part, wave, (front, back)[part])
-
-    for wave in (0, 1):
-        give("0", None, half, None, wave, right)
-        give("1", None, half, None, wave, left)
-        give("3", None, half, None, wave, below)
-        pass_on("own", None, None, None, wave)
+    targets = {0: right, 1: left, 3: below, 4: corners_below[1], 5: corners_below[0]}
+
+    def give_own(wave):
+        for index in DIRECT_SHARDS:
+            ref = piece(OWN, half, None, wave, core)
+            links.send((str(index), wave), ref, ref, targets[index])
+        pass_on("own", OWN, None, None, wave)
+
+    give_own(0)
 
     links.send("prev", frames.at[0], xs.at[pl.ds(ROWS, ROWS), :], later)
     links.send("next", frames.at[0, pl.ds(0, RIM), :], xs.at[pl.ds(2 * ROWS + RIM, RIM), :], earlier)
@@ -235,7 +252,7 @@
             mid[pl.ds(pl.multiple_of(first + 8, 8), size), :] = block
         return block
 
-    @pl.loop(0, 4)
+    @pl.loop(0, 4, unroll=True)
     def _(step):
         norm_rows(pl.multiple_of(step * 32, 32), 32, True)
 
@@ -268,45 +285,53 @@
     age_rows = offset + iota((ROWS + 8, 128), 0)
     age[...] = age_rows - start_of(age_rows)
 
+    give_own(1)
+
+    def pass_z(index, part, wave):
+        give(f"z{part}{index}", index, half, part, wave, front if (index, part) in FORWARD else back)
+
     for wave in (0, 1):
-        take("0", 0, half, None, wave)
-        give("20", 0, half, 0, wave, right)
-        take("1", 1, half, None, wave)
-        give("21", 1, half, 1, wave, left)
-        take("3", 3, half, None, wave)
-        give("4", 3, half, None, wave, right)
-        give("5", 3, half, None, wave, left)
-        for index in (0, 1, 3):
-            pass_z(index, (0, 1), wave)
+        for index in DIRECT_SHARDS:
+            take(str(index), index, half, None, wave)
+            if index in RELAYED:
+                further, part = RELAYED[index]
+                give(f"{further}{part}", index, half, part, wave, (right, left)[part])
+            if index in HALVED:
+                for part in (0, 1):
+                    pass_z(index, part, wave)
             pass_on(str(index), index, half, None, wave)
+        for index in LATER:
+            of_half = None if index == 3 else 1 - half
+            ref = piece(OWN, of_half, None, wave, core)
+            links.send((f"o{index}", wave), ref, ref, targets[index])
     for wave in (0, 1):
-        take("4", 4, half, None, wave)
-        give("60", 4, half, 0, wave, right)
-        take("5", 5, half, None, wave)
-        give("61", 5, half, 1, wave, left)
-        for part in (0, 1):
-            take(f"2{part}", 2, half, part, wave)
-            pass_z(2, (part,), wave)
-            pass_on(f"2{part}", 2, half, part, wave)
-        for index in (4, 5):
-            pass_z(index, (0, 1), wave)
-            pass_on(str(index), index, half, None, wave)
-    for wave in (0, 1):
-        for part in (0, 1):
-            take(f"6{part}", 6, half, part, wave)
-            pass_z(6, (part,), wave)
-            pass_on(f"6{part}", 6, half, part, wave)
-        for index in (0, 1, 3, 2, 4, 5, 6):
+        for index in FAR_SHARDS:
+            for part in (0, 1):
+                take(f"{index}{part}", index, half, part, wave)
+                pass_z(index, part, wave)
+                pass_on(f"{index}{part}", index, half, part, wave)
+
+    def take_rest(wave):
+        for index in LATER:
+            of_half = None if index == 3 else 1 - half
+            take(f"o{index}", index, of_half, None, wave)
+            pass_on(f"o{index}", index, of_half, None, wave)
+        for index in HALVED:
             for part in (0, 1):
                 take(f"z{part}{index}", index, 1 - half, part, wave)
                 pass_on(f"z{part}{index}", index, 1 - half, part, wave)
+
+    def take_siblings(of_wave):
+        for name, index, of_half, part, wave in siblings:
+            if wave == of_wave:
+                take("sib" + name, index, of_half, part, wave, 1 - core)
 
     links.arrived("prev", xs.at[pl.ds(ROWS, ROWS), :], earlier)
     links.arrived("next", xs.at[pl.ds(2 * ROWS + RIM, RIM), :], earlier)
     links.arrived("prev2", xs.at[pl.ds(2 * ROWS, RIM), :], earlier)
     links.arrived("cot", cts.at[pl.ds(ROWS, RIM), :], earlier)
 
-    @pl.loop(4, 8)
+    @pl.loop(4, 8, unroll=True)
     def _(step):
         norm_rows(pl.multiple_of(step * 32, 32), 32, False)
 
@@ -314,19 +339,19 @@
     mid[pl.ds(ROWS + 8, 8), :] = block[RIM : RIM + 8]
     mid[pl.ds(0, 8), :] = xs[pl.ds(2 * ROWS - RIM, RIM), :].astype(F32)[8:]
 
-    for name, index, of_half, part, wave in siblings:
-        take("sib" + name, index, of_half, part, wave, 1 - core)
+    take_rest(0)
+    take_siblings(0)
 
     normed = norm_b[...]
     keys[...] = dot(normed, weights[0]).astype(BF16)
-    values[...] = dot(normed, weights[1]).astype(BF16)
     rows = jnp.concatenate(
         [normed[:ROWS], normed[2 * ROWS - RIM : 2 * ROWS], normed[2 * ROWS + RIM :]], axis=0
     )
-    projected = dot(rows, weights[2])
+    projected = dot(rows, weights[1])
     query[...] = projected[:ROWS].astype(BF16)
     query_e[...] = projected[ROWS + 8 : ROWS + 24].astype(BF16)
     links.send("query", query, query_n, earlier)
+    take_rest(1)
 
     def head(index):
         return slice(index * HEAD_DIM, (index + 1) * HEAD_DIM)
@@ -338,15 +363,18 @@
         top = jnp.max(scores, axis=-1, keepdims=True)
         shifted = jnp.exp(scores - top)
         part = 1.0 / jnp.sum(shifted, axis=-1, keepdims=True)
-        share = shifted * part
-        probs[h] = share
-        context[8 : ROWS + 8, head(h)] = dot(share.astype(BF16), values[: 2 * ROWS, head(h)])
+        probs[h] = shifted * part
         columns = jnp.where(lane == h, top, columns)
         columns = jnp.where(lane == HEADS + h, part, columns)
         scores = dot_nt(query_e[:, head(h)], keys[:, head(h)]) * SCALE + mask_rim[...]
         shifted = jnp.exp(scores - jnp.max(scores, axis=-1, keepdims=True))
         share = shifted * (1.0 / jnp.sum(shifted, axis=-1, keepdims=True))
-        rims = dot(share.astype(BF16), values[:, head(h)])
+        probs_rim[h] = share.astype(BF16)
+    take_siblings(1)
+    values[...] = dot(norm_b[...], weights[2]).astype(BF16)
+    for h in range(HEADS):
+        context[8 : ROWS + 8, head(h)] = dot(probs[h].astype(BF16), values[: 2 * ROWS, head(h)])
+        rims = dot(probs_rim[h], values[:, head(h)])
         context[0:8, head(h)] = rims[:8]
         context[ROWS + 8 :, head(h)] = rims[8:]
     stats[...] = columns.T[:8]
@@ -354,7 +382,7 @@
 
     mid[...] += dot_nt(context[...].astype(BF16), weights[3])
 
-    @pl.loop(0, 3)
+    @pl.loop(0, 3, unroll=True)
     def _(step):
         part_rows = pl.ds(pl.multiple_of(step * 48, 8), 48)
         scaled, inverse = normalize(mid[part_rows, :])
@@ -392,20 +420,23 @@
         early[tile, 10:11, :] = jnp.sum(term, axis=0, keepdims=True)
         early[tile, 11:16, :] = jnp.zeros((5, 128), F32)
 
-    def collect(name, me, size, slots):
-        for step in range(1, size):
-            links.arrived((name, step), slots.at[shift(me, -step, size)], sibling)
+    def spread_out(name, slots, me, steps):
+        for step, _, device, _ in steps:
+            links.send((name, step), slots.at[me], slots.at[me], device)
+
+    def collect(name, slots, steps):
+        for step, _, _, source in steps:
+            links.arrived((name, step), slots.at[source], sibling)
         total = slots[0]
-        for index in range(1, size):
+        for index in range(1, slots.shape[0]):
             total = total + slots[index]
         return total
 
     early_x[group] = early[group]
-    for step in range(1, GROUP):
-        other, device = group_peer(step)
+    for step, other, device, _ in group_steps:
         links.send(("ex", step), early.at[other], early_x.at[group], device)
 
-    @pl.loop(0, 4)
+    @pl.loop(0, 4, unroll=True)
     def _(step):
         part_rows = pl.ds(pl.multiple_of(step * 32, 32), 32)
         ext_rows = pl.ds(pl.multiple_of(step * 32 + 8, 8), 32)
@@ -418,14 +449,10 @@
 
     grad_context[...] = dot(grad_mid_b[...], weights[3]).astype(BF16)
     links.send("grad", grad_context, grad_context_n, earlier)
-    columns = jnp.zeros(square, F32)
     deltas = []
     for h in range(HEADS):
         term = context[8 : ROWS + 8, head(h)] * grad_context[:, head(h)].astype(F32)
         deltas.append(jnp.sum(term, axis=-1, keepdims=True))
-        columns = jnp.where(lane == h, deltas[h], columns)
-    delta[...] = columns.T[:8]
-    links.send("delta", delta, delta_n, earlier)
 
     for h in range(HEADS):
         grad_h = grad_context[:, head(h)]
@@ -436,26 +463,28 @@
         grad_key[:, head(h)] = dot_tn(grad_scores, query[:, head(h)]).astype(BF16)
         grad_value[:, head(h)] = dot_tn(share.astype(BF16), grad_h).astype(BF16)
 
-    parts = dot_nt(grad_key[...], weights[0]) + dot_nt(grad_value[...], weights[1])
-    own_part = parts[:ROWS] + dot_nt(grad_query[...], weights[2])
+    parts = dot_nt(grad_key[...], weights[0]) + dot_nt(grad_value[...], weights[2])
+    own_part = parts[:ROWS] + dot_nt(grad_query[...], weights[1])
     grad_norm_a[...] = own_part
     product = own_part * scaled_a[:ROWS] + parts[ROWS:] * scaled_a[ROWS:]
     total = jnp.sum(product, axis=0, keepdims=True)
     for tile in range(WIDTH // 128):
         late_sum[tile : tile + 1, :] = total[:, tile * 128 : (tile + 1) * 128]
     late_x[group] = late_sum[...]
-    for step in range(1, GROUP):
-        links.send(("lx", step), late_x.at[group], late_x.at[group], group_peer(step)[1])
-
-    early_y[y] = collect("ex", group, GROUP, early_x)
-    for step in range(1, NY):
-        links.send(("ey", step), early_y.at[y], early_y.at[y], y_peer(step)[1])
-    late_y[y] = collect("lx", group, GROUP, late_x)
-    for step in range(1, NY):
-        links.send(("ly", step), late_y.at[y], late_y.at[y], y_peer(step)[1])
-    early_z[z] = collect("ey", y, NY, early_y)
-    for step in range(1, NZ):
-        links.send(("ez", step), early_z.at[z], early_z.at[z], z_peer(step)[1])
+    spread_out("lx", late_x, group, group_steps)
+
+    columns = jnp.zeros(square, F32)
+    for h in range(HEADS):
+        columns = jnp.where(lane == h, deltas[h], columns)
+    delta[...] = columns.T[:8]
+    links.send("delta", delta, delta_n, earlier)
+
+    early_z[z] = collect("ex", early_x, group_steps)
+    spread_out("ez", early_z, z, z_steps)
+    late_z[z] = collect("lx", late_x, group_steps)
+    spread_out("lz", late_z, z, z_steps)
+    early_y[y] = collect("ez", early_z, z_steps)
+    spread_out("ey", early_y, y, y_steps)
 
     links.arrived("query", query_n, earlier)
     links.arrived("stats", stats_n, earlier)
@@ -470,16 +499,14 @@
         grad_key[:ROWS, head(h)] = dot(grad_scores, query_h).astype(BF16)
         grad_value[:ROWS, head(h)] = dot(share.astype(BF16), grad_h).astype(BF16)
 
-    late_z[z] = collect("ly", y, NY, late_y)
-    for step in range(1, NZ):
-        links.send(("lz", step), late_z.at[z], late_z.at[z], z_peer(step)[1])
-    early_all[group] = collect("ez", z, NZ, early_z)
-    for step in range(1, GROUP):
-        links.send(("ea", step), early_all.at[group], early_all.at[group], group_peer(step)[1])
-
-    grad_norm_a[...] += dot_nt(grad_key[:ROWS], weights[0]) + dot_nt(grad_value[:ROWS], weights[1])
-
-    @pl.loop(0, 4)
+    late_y[y] = collect("lz", late_z, z_steps)
+    spread_out("ly", late_y, y, y_steps)
+    early_all[group] = collect("ey", early_y, y_steps)
+    spread_out("ea", early_all, group, group_steps)
+
+    grad_norm_a[...] += dot_nt(grad_key[:ROWS], weights[0]) + dot_nt(grad_value[:ROWS], weights[2])
+
+    @pl.loop(0, 4, unroll=True)
     def _(step):
         part_rows = pl.ds(pl.multiple_of(step * 32, 32), 32)
         grad, scaled = grad_norm_a[part_rows, :] * gain_a[...], scaled_a[part_rows, :]
@@ -492,11 +519,11 @@
     links.finish()
 
     factor = 1.0 / math.sqrt(NX * 2 * 2 * (NY // 2) * NZ * ROWS)
-    for step in range(1, GROUP):
-        links.arrived(("ea", step), early_all.at[shift(group, -step, GROUP)], sibling)
+    for step, _, _, source in group_steps:
+        links.arrived(("ea", step), early_all.at[source], sibling)
     for tile in range(WIDTH // 128):
         sums[:, tile * 128 : (tile + 1) * 128] = early_all[tile] * factor
-    summed = collect("lz", z, NZ, late_z) * factor
+    summed = collect("ly", late_y, y_steps) * factor
     for tile in range(WIDTH // 128):
         sums[11:12, tile * 128 : (tile + 1) * 128] = summed[tile : tile + 1]
     bring(sums, out_sums).wait()
@@ -535,6 +562,7 @@
         buffer(16, HEADS_WIDTH, dtype=BF16),
         buffer(ROWS, HEADS_WIDTH, dtype=BF16),
         buffer(HEADS, ROWS, 2 * ROWS),
+        buffer(HEADS, 16, EXT, dtype=BF16),
         buffer(CONV, HEADS_WIDTH),
         buffer(CONV, WIDTH),
         buffer(CONV, WIDTH),

time: 71 us -> 64.5 us (0.908)
  Pallas kernels: 70.2 us -> 63.7 us
    pallas_call x1, Pallas kernels: 68.3 us -> 61.8 us  [shards(): pl.pallas_call(block_kernel, out_shape=(jax.ShapeDtypeStruct(frames.shape...]
where the time goes in v3:
time: 64.5 us; the launch traced here: 64.3 us
  Pallas kernels  63.7 us (99%)
    pallas_call x1, Pallas kernels, shards(): pl.pallas_call(block_kernel, out_shape=(jax.ShapeDtypeStruct(frames.shape...  61.8 us
    pallas_call x1, Pallas kernels, shards(): pl.pallas_call(finish_kernel, grid=(steps,), out_shape=(jax.ShapeDtypeStr...  1.83 us

profile of v3, /device:TPU:1, one launch (start us, length us, event | category | flops | bytes accessed | tf_op | source)
XLA Modules:
  0.0 64.3 jit_solution(2128168918057368646)
XLA Ops:
  0.6 61.8 %shard_map.146 = (f32[1,128,1024]{2,1,0:T(8,128)}, f32[16,1024]{1,0:T(8,128)}) custom-call(bf16[1,128,1024]{2,1,0:T(8,128)(2,1)} %frames.1, bf16[1,128,1024]{2,1,0:T(8,128)(2,1)} %cotangent.1, s32[1,4]{1,0:T(1,128)} %lengths.1, bf16[64,512]{1,0:T(8,128)(2,1)} %w_query.1, bf16[64,512]{1,0:T(8,128)(2,1)} %w_key.1, bf16[64,512]{1,0:T(8,128)(2,1)} %w_value.1, ...), custom_call_target="tpu_custom_call" | custom-call | flops 3221225472 | bytes 4194304 | tf_op jit(solution)/shard_map/pallas_call | solution.py:613
  62.5 1.8 %shard_map.147 = (f32[1,128,1024]{2,1,0:T(8,128)}, f32[1,1024]{1,0:T(1,128)}, f32[1,1024]{1,0:T(1,128)}, f32[9,1024]{1,0:T(8,128)}, f32[1,1024]{1,0:T(1,128)}) custom-call(f32[1,128,1024]{2,1,0:T(8,128)} %get-tuple-element.12.frames_in, f32[16,1024]{1,0:T(8,128)} %get-tuple-element.13.sums), custom_call_target="tpu_custom_call" | custom-call | tf_op jit(solution)/shard_map/pallas_call | solution.py:638

commit v4 on v3

--- a/solution.py
+++ b/solution.py
@@ -98,7 +98,7 @@
 def block_kernel(
     frames, cotangent, lengths, w_query, w_key, w_value, w_output, att_gain, conv_gain, kernel, bias,
     out_frames, out_sums,
-    xs, cts, weights, gain_a, gain_c, taps_ref, bias_ref,
+    xs, cts, rims_out, rims_in, weights, gain_a, gain_c, taps_ref, bias_ref,
     norm_b, scaled_a, inverse_a, keys, values, query, query_e, query_n, probs, probs_rim, context, mid,
     scaled_c, inverse_c, conv_in, age, grad_conv, grad_conv_in, grad_mid_norm, grad_mid_b,
     grad_context, grad_context_n, grad_query, grad_key, grad_value, grad_norm_a,
@@ -170,7 +170,7 @@
         return copy
 
     barrier = pltpu.get_barrier_semaphore()
-    peers = [step[2] for step in group_steps + y_steps + z_steps]
+    peers = [step[2] for step in z_steps + y_steps + group_steps]
     peers += [later, earlier, later_2, frames_at(-2)]
     peers += corners_above + corners_below
     for peer in peers:
@@ -192,6 +192,20 @@
 
     for copy in got_weights:
         copy.wait()
+    got_frames.wait()
+    for copy in got_rest:
+        copy.wait()
+
+    def pack(rows):
+        return jnp.concatenate([rows[:, : WIDTH // 2], rows[:, WIDTH // 2 :]], axis=0).astype(BF16)
+
+    def unpack(packed):
+        rows = packed.astype(F32)
+        return jnp.concatenate([rows[:8], rows[8:]], axis=1)
+
+    rims_out[0] = pack(xs[ROWS - RIM : ROWS, :].astype(F32)[8:])
+    rims_out[1] = pack(xs[:RIM, :].astype(F32)[:8])
+    rims_out[2] = pack(cts[:RIM, :].astype(F32)[:8])
     pl.semaphore_wait(barrier, len(peers))
 
     half = z - 2 * lax.div(z, 2)
@@ -206,7 +220,7 @@
             first, size = first + of_half * 32, 32
         if part is not None:
             first, size = first + part * 16, 16
-        return weights.at[pl.ds(2 * wave, 2), pl.ds(pl.multiple_of(first, 16), size), :]
+        return weights.at[:, pl.ds(pl.multiple_of(first, 16), size), :]
 
     def give(name, index, of_half, part, wave, device):
         ref = piece(index, of_half, part, wave, core)
@@ -233,13 +247,9 @@
     give_own(0)
 
     links.send("prev", frames.at[0], xs.at[pl.ds(ROWS, ROWS), :], later)
-    links.send("next", frames.at[0, pl.ds(0, RIM), :], xs.at[pl.ds(2 * ROWS + RIM, RIM), :], earlier)
-    links.send("prev2", frames.at[0, pl.ds(ROWS - RIM, RIM), :], xs.at[pl.ds(2 * ROWS, RIM), :], later_2)
-    links.send("cot", cotangent.at[0, pl.ds(0, RIM), :], cts.at[pl.ds(ROWS, RIM), :], earlier)
-
-    got_frames.wait()
-    for copy in got_rest:
-        copy.wait()
+    links.send("prev2", rims_out.at[0], rims_in.at[0], later_2)
+    links.send("next", rims_out.at[1], rims_in.at[1], earlier)
+    links.send("cot", rims_out.at[2], rims_in.at[2], earlier)
 
     def norm_rows(first, size, own):
         block = xs[pl.ds(first, size), :].astype(F32)
@@ -285,12 +295,11 @@
     age_rows = offset + iota((ROWS + 8, 128), 0)
     age[...] = age_rows - start_of(age_rows)
 
-    give_own(1)
 
     def pass_z(index, part, wave):
         give(f"z{part}{index}", index, half, part, wave, front if (index, part) in FORWARD else back)
 
-    for wave in (0, 1):
+    for wave in (0,):
         for index in DIRECT_SHARDS:
             take(str(index), index, half, None, wave)
             if index in RELAYED:
@@ -304,7 +313,7 @@
             of_half = None if index == 3 else 1 - half
             ref = piece(OWN, of_half, None, wave, core)
             links.send((f"o{index}", wave), ref, ref, targets[index])
-    for wave in (0, 1):
+    for wave in (0,):
         for index in FAR_SHARDS:
             for part in (0, 1):
                 take(f"{index}{part}", index, half, part, wave)
@@ -327,9 +336,14 @@
                 take("sib" + name, index, of_half, part, wave, 1 - core)
 
     links.arrived("prev", xs.at[pl.ds(ROWS, ROWS), :], earlier)
-    links.arrived("next", xs.at[pl.ds(2 * ROWS + RIM, RIM), :], earlier)
-    links.arrived("prev2", xs.at[pl.ds(2 * ROWS, RIM), :], earlier)
-    links.arrived("cot", cts.at[pl.ds(ROWS, RIM), :], earlier)
+    links.arrived("prev2", rims_in.at[0], earlier)
+    links.arrived("next", rims_in.at[1], earlier)
+    links.arrived("cot", rims_in.at[2], earlier)
+    zeros = jnp.zeros((8, WIDTH), F32)
+    before, after, cot_after = (unpack(rims_in[index]) for index in range(3))
+    xs[2 * ROWS : 2 * ROWS + RIM, :] = jnp.concatenate([zeros, before], axis=0).astype(BF16)
+    xs[2 * ROWS + RIM :, :] = jnp.concatenate([after, zeros], axis=0).astype(BF16)
+    cts[ROWS:, :] = jnp.concatenate([cot_after, zeros], axis=0).astype(BF16)
 
     @pl.loop(4, 8, unroll=True)
     def _(step):
@@ -351,7 +365,6 @@
     query[...] = projected[:ROWS].astype(BF16)
     query_e[...] = projected[ROWS + 8 : ROWS + 24].astype(BF16)
     links.send("query", query, query_n, earlier)
-    take_rest(1)
 
     def head(index):
         return slice(index * HEAD_DIM, (index + 1) * HEAD_DIM)
@@ -370,7 +383,6 @@
         shifted = jnp.exp(scores - jnp.max(scores, axis=-1, keepdims=True))
         share = shifted * (1.0 / jnp.sum(shifted, axis=-1, keepdims=True))
         probs_rim[h] = share.astype(BF16)
-    take_siblings(1)
     values[...] = dot(norm_b[...], weights[2]).astype(BF16)
     for h in range(HEADS):
         context[8 : ROWS + 8, head(h)] = dot(probs[h].astype(BF16), values[: 2 * ROWS, head(h)])
@@ -548,6 +560,8 @@
     return [
         buffer(EXT, WIDTH, dtype=BF16),
         buffer(CONV, WIDTH, dtype=BF16),
+        buffer(3, 16, WIDTH // 2, dtype=BF16),
+        buffer(3, 16, WIDTH // 2, dtype=BF16),
         buffer(4, WIDTH, HEADS_WIDTH, dtype=BF16),
         buffer(1, WIDTH),
         buffer(1, WIDTH),

time: 64.5 us -> 61.8 us (0.958)
  Pallas kernels: 63.7 us -> 61 us
    pallas_call x1, Pallas kernels: 61.8 us -> 59.1 us  [shards(): pl.pallas_call(block_kernel, out_shape=(jax.ShapeDtypeStruct(frames.shape...]
where the time goes in v4:
time: 61.8 us; the launch traced here: 61.6 us
  Pallas kernels  61 us (99%)
  between operations  0.64 us (1%)
    pallas_call x1, Pallas kernels, shards(): pl.pallas_call(block_kernel, out_shape=(jax.ShapeDtypeStruct(frames.shape...  59.1 us
    pallas_call x1, Pallas kernels, shards(): pl.pallas_call(finish_kernel, grid=(steps,), out_shape=(jax.ShapeDtypeStr...  1.83 us

profile of v4, /device:TPU:1, one launch (start us, length us, event | category | flops | bytes accessed | tf_op | source)
XLA Modules:
  0.0 61.6 jit_solution(2638376471711714546)
XLA Ops:
  0.6 59.1 %shard_map.146 = (f32[1,128,1024]{2,1,0:T(8,128)}, f32[16,1024]{1,0:T(8,128)}) custom-call(bf16[1,128,1024]{2,1,0:T(8,128)(2,1)} %frames.1, bf16[1,128,1024]{2,1,0:T(8,128)(2,1)} %cotangent.1, s32[1,4]{1,0:T(1,128)} %lengths.1, bf16[64,512]{1,0:T(8,128)(2,1)} %w_query.1, bf16[64,512]{1,0:T(8,128)(2,1)} %w_key.1, bf16[64,512]{1,0:T(8,128)(2,1)} %w_value.1, ...), custom_call_target="tpu_custom_call" | custom-call | flops 3221225472 | bytes 4194304 | tf_op jit(solution)/shard_map/pallas_call | solution.py:627
  59.8 1.8 %shard_map.147 = (f32[1,128,1024]{2,1,0:T(8,128)}, f32[1,1024]{1,0:T(1,128)}, f32[1,1024]{1,0:T(1,128)}, f32[9,1024]{1,0:T(8,128)}, f32[1,1024]{1,0:T(1,128)}) custom-call(f32[1,128,1024]{2,1,0:T(8,128)} %get-tuple-element.12.frames_in, f32[16,1024]{1,0:T(8,128)} %get-tuple-element.13.sums), custom_call_target="tpu_custom_call" | custom-call | tf_op jit(solution)/shard_map/pallas_call | solution.py:652

commit v5 on v4

--- a/solution.py
+++ b/solution.py
@@ -102,8 +102,8 @@
     norm_b, scaled_a, inverse_a, keys, values, query, query_e, query_n, probs, probs_rim, context, mid,
     scaled_c, inverse_c, conv_in, age, grad_conv, grad_conv_in, grad_mid_norm, grad_mid_b,
     grad_context, grad_context_n, grad_query, grad_key, grad_value, grad_norm_a,
-    frames_out, mask_main, mask_rim, mask_next, stats, stats_n, delta, delta_n,
-    early, early_x, early_y, early_z, early_all, late_sum, late_x, late_y, late_z,
+    frames_out, mask_main, mask_rim, mask_next, stats, stats_n,
+    early, early_b, early_x, early_y, early_z, early_all, late_sum, late_x, late_y, late_z,
     sums,
     send_sems, recv_sems, local_sems,
 ):
@@ -335,6 +335,8 @@
             if wave == of_wave:
                 take("sib" + name, index, of_half, part, wave, 1 - core)
 
+    take_rest(0)
+
     links.arrived("prev", xs.at[pl.ds(ROWS, ROWS), :], earlier)
     links.arrived("prev2", rims_in.at[0], earlier)
     links.arrived("next", rims_in.at[1], earlier)
@@ -353,7 +355,6 @@
     mid[pl.ds(ROWS + 8, 8), :] = block[RIM : RIM + 8]
     mid[pl.ds(0, 8), :] = xs[pl.ds(2 * ROWS - RIM, RIM), :].astype(F32)[8:]
 
-    take_rest(0)
     take_siblings(0)
 
     normed = norm_b[...]
@@ -369,16 +370,15 @@
     def head(index):
         return slice(index * HEAD_DIM, (index + 1) * HEAD_DIM)
 
-    lane = iota(square, 1)
-    columns = jnp.zeros(square, F32)
+    tops, shares = [], []
     for h in range(HEADS):
         scores = dot_nt(query[:, head(h)], keys[: 2 * ROWS, head(h)]) * SCALE + mask_main[...]
         top = jnp.max(scores, axis=-1, keepdims=True)
         shifted = jnp.exp(scores - top)
         part = 1.0 / jnp.sum(shifted, axis=-1, keepdims=True)
         probs[h] = shifted * part
-        columns = jnp.where(lane == h, top, columns)
-        columns = jnp.where(lane == HEADS + h, part, columns)
+        tops.append(top)
+        shares.append(part)
         scores = dot_nt(query_e[:, head(h)], keys[:, head(h)]) * SCALE + mask_rim[...]
         shifted = jnp.exp(scores - jnp.max(scores, axis=-1, keepdims=True))
         share = shifted * (1.0 / jnp.sum(shifted, axis=-1, keepdims=True))
@@ -389,8 +389,6 @@
         rims = dot(probs_rim[h], values[:, head(h)])
         context[0:8, head(h)] = rims[:8]
         context[ROWS + 8 :, head(h)] = rims[8:]
-    stats[...] = columns.T[:8]
-    links.send("stats", stats, stats_n, earlier)
 
     mid[...] += dot_nt(context[...].astype(BF16), weights[3])
 
@@ -439,14 +437,15 @@
     def collect(name, slots, steps):
         for step, _, _, source in steps:
             links.arrived((name, step), slots.at[source], sibling)
-        total = slots[0]
+        total = slots[0].astype(F32)
         for index in range(1, slots.shape[0]):
-            total = total + slots[index]
+            total = total + slots[index].astype(F32)
         return total
 
-    early_x[group] = early[group]
+    early_b[...] = early[...].astype(BF16)
+    early_x[group] = early_b[group]
     for step, other, device, _ in group_steps:
-        links.send(("ex", step), early.at[other], early_x.at[group], device)
+        links.send(("ex", step), early_b.at[other], early_x.at[group], device)
 
     @pl.loop(0, 4, unroll=True)
     def _(step):
@@ -485,35 +484,35 @@
     late_x[group] = late_sum[...]
     spread_out("lx", late_x, group, group_steps)
 
+    lane = iota(square, 1)
     columns = jnp.zeros(square, F32)
-    for h in range(HEADS):
-        columns = jnp.where(lane == h, deltas[h], columns)
-    delta[...] = columns.T[:8]
-    links.send("delta", delta, delta_n, earlier)
-
-    early_z[z] = collect("ex", early_x, group_steps)
+    for index, column in enumerate(tops + shares + deltas):
+        columns = jnp.where(lane == index, column, columns)
+    stats[...] = columns.T[:16]
+    links.send("stats", stats, stats_n, earlier)
+
+    early_z[z] = collect("ex", early_x, group_steps).astype(BF16)
     spread_out("ez", early_z, z, z_steps)
     late_z[z] = collect("lx", late_x, group_steps)
     spread_out("lz", late_z, z, z_steps)
-    early_y[y] = collect("ez", early_z, z_steps)
+    early_y[y] = collect("ez", early_z, z_steps).astype(BF16)
     spread_out("ey", early_y, y, y_steps)
 
     links.arrived("query", query_n, earlier)
     links.arrived("stats", stats_n, earlier)
     links.arrived("grad", grad_context_n, earlier)
-    links.arrived("delta", delta_n, earlier)
     for h in range(HEADS):
         query_h, grad_h = query_n[:, head(h)], grad_context_n[:, head(h)]
         scores = dot_nt(keys[:ROWS, head(h)], query_h) * SCALE + mask_next[...]
         share = jnp.exp(scores - stats_n[h : h + 1, :]) * stats_n[HEADS + h : HEADS + h + 1, :]
         grad_probs = dot_nt(values[:ROWS, head(h)], grad_h)
-        grad_scores = (share * (grad_probs - delta_n[h : h + 1, :]) * SCALE).astype(BF16)
+        grad_scores = (share * (grad_probs - stats_n[2 * HEADS + h : 2 * HEADS + h + 1, :]) * SCALE).astype(BF16)
         grad_key[:ROWS, head(h)] = dot(grad_scores, query_h).astype(BF16)
         grad_value[:ROWS, head(h)] = dot(share.astype(BF16), grad_h).astype(BF16)
 
     late_y[y] = collect("lz", late_z, z_steps)
     spread_out("ly", late_y, y, y_steps)
-    early_all[group] = collect("ey", early_y, y_steps)
+    early_all[group] = collect("ey", early_y, y_steps).astype(BF16)
     spread_out("ea", early_all, group, group_steps)
 
     grad_norm_a[...] += dot_nt(grad_key[:ROWS], weights[0]) + dot_nt(grad_value[:ROWS], weights[2])
@@ -534,7 +533,7 @@
     for step, _, _, source in group_steps:
         links.arrived(("ea", step), early_all.at[source], sibling)
     for tile in range(WIDTH // 128):
-        sums[:, tile * 128 : (tile + 1) * 128] = early_all[tile] * factor
+        sums[:, tile * 128 : (tile + 1) * 128] = early_all[tile].astype(F32) * factor
     summed = collect("ly", late_y, y_steps) * factor
     for tile in range(WIDTH // 128):
         sums[11:12, tile * 128 : (tile + 1) * 128] = summed[tile : tile + 1]
@@ -597,15 +596,14 @@
         buffer(ROWS, 2 * ROWS),
         buffer(16, EXT),
         buffer(ROWS, ROWS),
-        buffer(8, 128),
-        buffer(8, 128),
-        buffer(8, 128),
-        buffer(8, 128),
+        buffer(16, 128),
+        buffer(16, 128),
         buffer(GROUP, 16, 128),
-        buffer(GROUP, 16, 128),
-        buffer(NY, 16, 128),
-        buffer(NZ, 16, 128),
-        buffer(GROUP, 16, 128),
+        buffer(GROUP, 16, 128, dtype=BF16),
+        buffer(GROUP, 16, 128, dtype=BF16),
+        buffer(NY, 16, 128, dtype=BF16),
+        buffer(NZ, 16, 128, dtype=BF16),
+        buffer(GROUP, 16, 128, dtype=BF16),
         buffer(8, 128),
         buffer(GROUP, 8, 128),
         buffer(NY, 8, 128),

time: 61.8 us -> 61 us (0.987)
  Pallas kernels: 61 us -> 60.2 us
    pallas_call x1, Pallas kernels: 59.1 us -> 58.4 us  [shards(): pl.pallas_call(block_kernel, out_shape=(jax.ShapeDtypeStruct(frames.shape...]
where the time goes in v5:
time: 61 us; the launch traced here: 60.8 us
  Pallas kernels  60.2 us (99%)
  between operations  0.64 us (1%)
    pallas_call x1, Pallas kernels, shards(): pl.pallas_call(block_kernel, out_shape=(jax.ShapeDtypeStruct(frames.shape...  58.4 us
    pallas_call x1, Pallas kernels, shards(): pl.pallas_call(finish_kernel, grid=(steps,), out_shape=(jax.ShapeDtypeStr...  1.83 us

profile of v5, /device:TPU:1, one launch (start us, length us, event | category | flops | bytes accessed | tf_op | source)
XLA Modules:
  0.0 60.8 jit_solution(15280512320250238096)
XLA Ops:
  0.6 58.4 %shard_map.146 = (f32[1,128,1024]{2,1,0:T(8,128)}, f32[16,1024]{1,0:T(8,128)}) custom-call(bf16[1,128,1024]{2,1,0:T(8,128)(2,1)} %frames.1, bf16[1,128,1024]{2,1,0:T(8,128)(2,1)} %cotangent.1, s32[1,4]{1,0:T(1,128)} %lengths.1, bf16[64,512]{1,0:T(8,128)(2,1)} %w_query.1, bf16[64,512]{1,0:T(8,128)(2,1)} %w_key.1, bf16[64,512]{1,0:T(8,128)(2,1)} %w_value.1, ...), custom_call_target="tpu_custom_call" | custom-call | flops 3221225472 | bytes 4194304 | tf_op jit(solution)/shard_map/pallas_call | solution.py:625
  59.0 1.8 %shard_map.147 = (f32[1,128,1024]{2,1,0:T(8,128)}, f32[1,1024]{1,0:T(1,128)}, f32[1,1024]{1,0:T(1,128)}, f32[9,1024]{1,0:T(8,128)}, f32[1,1024]{1,0:T(1,128)}) custom-call(f32[1,128,1024]{2,1,0:T(8,128)} %get-tuple-element.12.frames_in, f32[16,1024]{1,0:T(8,128)} %get-tuple-element.13.sums), custom_call_target="tpu_custom_call" | custom-call | tf_op jit(solution)/shard_map/pallas_call | solution.py:650

commit v6 on v5

--- a/solution.py
+++ b/solution.py
@@ -246,10 +246,10 @@
 
     give_own(0)
 
-    links.send("prev", frames.at[0], xs.at[pl.ds(ROWS, ROWS), :], later)
     links.send("prev2", rims_out.at[0], rims_in.at[0], later_2)
     links.send("next", rims_out.at[1], rims_in.at[1], earlier)
     links.send("cot", rims_out.at[2], rims_in.at[2], earlier)
+    links.send("prev", frames.at[0], xs.at[pl.ds(ROWS, ROWS), :], later)
 
     def norm_rows(first, size, own):
         block = xs[pl.ds(first, size), :].astype(F32)

time: 61 us -> 61 us (level)
  no operation moved by 1% of the time
where the time goes in v6:
time: 61 us; the launch traced here: 60.8 us
  Pallas kernels  60.2 us (99%)
  between operations  0.64 us (1%)
    pallas_call x1, Pallas kernels, shards(): pl.pallas_call(block_kernel, out_shape=(jax.ShapeDtypeStruct(frames.shape...  58.4 us
    pallas_call x1, Pallas kernels, shards(): pl.pallas_call(finish_kernel, grid=(steps,), out_shape=(jax.ShapeDtypeStr...  1.83 us

profile of v6, /device:TPU:1, one launch (start us, length us, event | category | flops | bytes accessed | tf_op | source)
XLA Modules:
  0.0 60.8 jit_solution(14432844883808657989)
XLA Ops:
  0.6 58.4 %shard_map.146 = (f32[1,128,1024]{2,1,0:T(8,128)}, f32[16,1024]{1,0:T(8,128)}) custom-call(bf16[1,128,1024]{2,1,0:T(8,128)(2,1)} %frames.1, bf16[1,128,1024]{2,1,0:T(8,128)(2,1)} %cotangent.1, s32[1,4]{1,0:T(1,128)} %lengths.1, bf16[64,512]{1,0:T(8,128)(2,1)} %w_query.1, bf16[64,512]{1,0:T(8,128)(2,1)} %w_key.1, bf16[64,512]{1,0:T(8,128)(2,1)} %w_value.1, ...), custom_call_target="tpu_custom_call" | custom-call | flops 3221225472 | bytes 4194304 | tf_op jit(solution)/shard_map/pallas_call | solution.py:625
  59.0 1.8 %shard_map.147 = (f32[1,128,1024]{2,1,0:T(8,128)}, f32[1,1024]{1,0:T(1,128)}, f32[1,1024]{1,0:T(1,128)}, f32[9,1024]{1,0:T(8,128)}, f32[1,1024]{1,0:T(1,128)}) custom-call(f32[1,128,1024]{2,1,0:T(8,128)} %get-tuple-element.12.frames_in, f32[16,1024]{1,0:T(8,128)} %get-tuple-element.13.sums), custom_call_target="tpu_custom_call" | custom-call | tf_op jit(solution)/shard_map/pallas_call | solution.py:650
